TPU v7x, 128 devices: a whole 4x4x4 slice. The times are simulated.
128 devices in a mesh: sec: 4 (over x_hi, core), dev: 32 (over x_lo, y, z).
Axes of the slice: x: 4 (x_hi: 2, x_lo: 2; x = x_hi * 2 + x_lo), y: 4, z: 4, core: 2. Of those that a mesh axis runs over, the one named last changes fastest.
Arguments:
- query_latent: bfloat16 [512, 128, 512], P('dev', 'sec'), may hold values from -60 to 60
- query_rope: bfloat16 [512, 8192], P('dev', 'sec'), may hold values from -5 to 5
- cache_latent: bfloat16 [512, 512, 512], P('dev'), may hold values from -5 to 5
- cache_rope: bfloat16 [512, 64, 512], P('dev'), may hold values from -5 to 5
- lengths: int32 [512], P('dev'), may hold values from 2 to 512
- value_up: bfloat16 [128, 512, 128], P('sec'), may hold values from -1 to 1
- output_proj: bfloat16 [16384, 7168], P('sec', 'dev'), may hold values from -0.046875 to 0.046875
- hidden: bfloat16 [512, 7168], P(None, 'dev'), may hold values from -6 to 6
- norm_gain: float32 [7168], replicated, may hold values from 0.1 to 1.9
- route_ids: int32 [512, 8], replicated, may hold values from 0 to 31, all different within a row; in each aligned block of 512 rows (0 to 511, 512 to 1023, ...) at most 256 rows name the same one
- route_weights: float32 [512, 8], replicated, may hold values from 0.1 to 0.5
- gate_proj: bfloat16 [32, 7168, 1024], P('dev', None, 'sec'), may hold values from -0.0625 to 0.0625
- up_proj: bfloat16 [32, 7168, 1024], P('dev', None, 'sec'), may hold values from -0.0625 to 0.0625
- down_proj: bfloat16 [32, 1024, 7168], P('dev', 'sec'), may hold values from -0.1875 to 0.1875
Outputs:
- mixed_out: bfloat16 [512, 7168], P('sec', 'dev')
Inputs may be any that keep to these rules, and one draw needn't show every extreme that they name: `route_ids`: each user names 8 different experts; no expert is named by more than 256 users, a bound that some block reaches.
All inputs are finite; a program needn't handle non-finite values.
Results may differ from a plain program's by a relative error of at most 0.008.
Values may be sent and summed in bfloat16 or wider, within the bound.
A program may use at most 128 MiB of HBM per device.

v0:
```python
import jax
import jax.numpy as jnp
from jax import lax
from jax.sharding import PartitionSpec as P

ROPE = 64
NOPE = 128


norm_eps = 1e-06


def expert_partial(arrived_rows, norm_gain, gate_w, up_w, down_w):
    values = arrived_rows.astype(jnp.float32)
    mean_square = jnp.mean(values * values, axis=-1, keepdims=True)
    normed = (values * lax.rsqrt(mean_square + norm_eps) * norm_gain).astype(jnp.bfloat16)
    gate = jnp.dot(normed, gate_w, preferred_element_type=jnp.float32)
    upward = jnp.dot(normed, up_w, preferred_element_type=jnp.float32)
    activation = (jax.nn.silu(gate) * upward).astype(jnp.bfloat16)
    return jnp.dot(activation, down_w, preferred_element_type=jnp.float32).astype(jnp.bfloat16)


def combine_users(returned, flat_index, route_weights):
    total_rows, topk = route_weights.shape
    columns = returned.shape[-1]
    picked = returned.reshape(-1, columns)[flat_index].reshape(total_rows, topk, columns)
    return jnp.sum(picked * route_weights[:, :, None], axis=1)


def body(
    query_latent,
    query_rope,
    cache_latent,
    cache_rope,
    lengths,
    value_up,
    output_proj,
    hidden,
    norm_gain,
    route_ids,
    route_weights,
    gate_proj,
    up_proj,
    down_proj,
):
    users_here, heads_here, latent_width = query_latent.shape
    history = cache_latent.shape[1]
    rope_width = cache_rope.shape[1]
    positional = query_rope.reshape(users_here, heads_here, rope_width)
    scores = jnp.einsum(
        "rhc,rtc->rht", query_latent, cache_latent, preferred_element_type=jnp.float32
    )
    scores = scores + jnp.einsum(
        "rhe,ret->rht", positional, cache_rope, preferred_element_type=jnp.float32
    )
    scores = scores * (NOPE + ROPE) ** (-0.5)
    visible = jnp.arange(history, dtype=jnp.int32)[None, None, :] < lengths[:, None, None]
    scores = jnp.where(visible, scores, -1e30)
    highest = jnp.max(scores, axis=-1, keepdims=True)
    exponent = jnp.exp(scores - highest)
    attn_weights = (exponent / jnp.sum(exponent, axis=-1, keepdims=True)).astype(jnp.bfloat16)
    context = jnp.einsum(
        "rht,rtc->rhc", attn_weights, cache_latent, preferred_element_type=jnp.float32
    ).astype(jnp.bfloat16)
    head_values = jnp.einsum(
        "rhc,hcv->rhv", context, value_up, preferred_element_type=jnp.float32
    ).astype(jnp.bfloat16)
    head_values = head_values.reshape(users_here, -1)
    partial_attn = jnp.dot(
        lax.all_gather(head_values, "dev", axis=0, tiled=True),
        output_proj,
        preferred_element_type=jnp.float32,
    )
    attn_out = lax.psum(partial_attn, "sec")
    residual = hidden.astype(jnp.float32) + attn_out
    routed = residual.astype(jnp.bfloat16)
    total_rows, columns = routed.shape
    topk = route_ids.shape[1]
    experts = gate_proj.shape[0] * lax.axis_size("dev")
    capacity = min(total_rows, 2 * total_rows * topk // experts)
    expert_ids = route_ids.reshape(-1)
    onehot = (expert_ids[:, None] == jnp.arange(experts, dtype=jnp.int32)[None, :]).astype(
        jnp.int32
    )
    earlier = jnp.cumsum(onehot, axis=0) - onehot
    slot_rank = jnp.sum(earlier * onehot, axis=1)
    pair_rows = jnp.arange(total_rows * topk, dtype=jnp.int32) // topk
    slot_rows = (
        jnp.full((experts, capacity), total_rows, jnp.int32)
        .at[expert_ids, slot_rank]
        .set(pair_rows)
    )
    flat_index = expert_ids * capacity + slot_rank
    padded = jnp.concatenate([routed, jnp.zeros((1, columns), jnp.bfloat16)], axis=0)
    outgoing = padded[slot_rows]
    sections = lax.axis_size("sec")
    section = lax.axis_index("sec")
    arrived = lax.all_to_all(outgoing, "dev", split_axis=0, concat_axis=2, tiled=True)
    partial_value = expert_partial(arrived[0], norm_gain, gate_proj[0], up_proj[0], down_proj[0])
    my_users = total_rows // sections
    row_start = section * my_users
    summed = lax.psum(partial_value.astype(jnp.float32).astype(jnp.bfloat16), "sec").astype(
        jnp.float32
    )
    returned = lax.all_to_all(summed[None], "dev", split_axis=2, concat_axis=0, tiled=True)
    expert_mix = combine_users(returned, flat_index, route_weights)
    result = lax.dynamic_slice_in_dim(residual + expert_mix, row_start, my_users, 0)
    return result.astype(jnp.bfloat16)


def solution(mesh):
    return jax.shard_map(
        body,
        mesh=mesh,
        in_specs=(
            P("dev", "sec", None),
            P("dev", "sec"),
            P("dev", None, None),
            P("dev", None, None),
            P("dev"),
            P("sec", None, None),
            P("sec", "dev"),
            P(None, "dev"),
            P(),
            P(),
            P(),
            P("dev", None, "sec"),
            P("dev", None, "sec"),
            P("dev", "sec", None),
        ),
        out_specs=P("sec", "dev"),
        check_vma=False,
    )
```

profile of v0, /device:TPU:0, one launch (start us, length us, event | category | flops | bytes accessed | tf_op | source)
XLA Modules:
  0.0 612.0 jit_solution(17372833025529411936)
XLA Ops:
  6.5 0.0 copy-start
  6.5 0.0 all-gather.2.cloned.1.call-start
  6.5 1.2 reshape.163
  7.7 0.7 iota_compare_fusion.2
  8.4 6.2 %fusion.41 = f32[16,32,512]{2,1,0:T(8,128)S(1)} fusion(bf16[16,32,512]{2,1,0:T(8,128)(2,1)} %param.14, bf16[16,512,512]{2,1,0:T(8,128)(2,1)} %param.16), kind=kOutput, calls=%fused_computation.71 | convolution fusion | flops 268435456 | bytes 9961472 | tf_op jit(solution)/shard_map/rhc,rtc->rht/dot_general | solution.py:50
  14.6 0.0 copy-done.4
  14.6 0.3 fusion.14
  14.9 0.3 fusion.40
  15.3 5.0 convolution_convert_fusion.1
  20.2 0.0 copy-start.7
  20.2 0.0 copy-start.10
  20.3 0.0 copy-start.9
  20.3 3.1 fusion.21
  23.3 0.7 copy.48
  24.0 0.0 all-gather.2.cloned.1.call-update
  24.0 0.0 all-reduce.4.cloned.1.call-start
  24.1 0.0 copy-done.7
  24.1 0.1 copy.29
  24.2 0.2 eq.29
  24.4 0.1 eq.25
  24.5 0.2 reshape.165
  24.7 0.1 fusion.27
  24.7 9.2 %reduce-window.6 = s32[32,32,128]{2,1,0:T(8,128)S(1)} reduce-window(s32[32,32,128]{2,1,0:T(8,128)S(1)} %fusion.27, s32[]{:T(128)} %constant.20.clone.1), window={size=1x1x128 pad=0_0x0_0x127_0}, to_apply=%region_3.4 | reduce-window | flops 16646144 | bytes 1048580 | tf_op jit(solution)/shard_map/reduce-window
  34.0 0.8 slice_reduce_fusion
  34.8 0.2 reduce-window.9
  34.9 0.2 broadcast_add_fusion
  35.2 0.4 fusion.24
  35.5 0.0 copy-start.5
  35.6 0.1 compare_select_fusion
  35.6 0.0 copy-done.10
  35.6 0.1 multiply_reduce_fusion
  35.8 0.1 and_reduce_fusion
  35.9 148.3 %all-gather.2.cloned.1.call-done = bf16[512,4096]{1,0:T(8,128)(2,1)} async-done(((bf16[16,4096]{1,0:T(8,128)(2,1)}), bf16[512,4096]{1,0:T(8,128)(2,1)}) %all-gather.2.cloned.1.call-update) | async-done | bytes 4194320 | tf_op jit(solution)/shard_map/all_gather | solution.py:70
  184.2 4.4 fusion.42
  188.6 0.0 all-reduce.4.cloned.1.call-update
  188.7 15.5 %scatter_custom_fusion = s32[8192]{0:T(1024)S(1)} fusion(s32[4096]{0:T(1024)S(1)} %get-tuple-element.11, s32[4096]{0:T(1024)S(1)} %get-tuple-element.10, s32[]{:T(128)} %constant.26.clone.1), kind=kCustom, calls=%fused_computation.60 | custom fusion | bytes 32772
  204.3 25.9 %all-reduce.4.cloned.1.call-done = f32[512,224]{0,1:T(8,128)} async-done(((f32[512,224]{0,1:T(8,128)}), f32[512,224]{0,1:T(8,128)}) %all-reduce.4.cloned.1.call-update) | async-done | bytes 458768 | tf_op jit(solution)/shard_map/psum | solution.py:74
  230.2 0.0 copy-done.5
  230.2 1.1 fusion.39
  231.3 0.1 copy.39
  231.5 32.9 %gather_fusion = bf16[8192,224]{1,0:T(8,128)(2,1)} fusion(bf16[513,224]{1,0:T(8,128)(2,1)S(1)} %concatenate.6.clone, s32[8192]{0:T(1024)S(1)} %broadcast_clamp_fusion), kind=kCustom, calls=%fused_computation | custom fusion | bytes 7372800 | tf_op jit(solution)/shard_map/gather | solution.py:95
  264.4 6.4 %copy.33 = bf16[32,256,224]{1,2,0:T(8,128)(2,1)} copy(bf16[32,256,224]{2,1,0:T(8,128)(2,1)} %bitcast.78) | data formatting | bytes 7340032 | tf_op jit(solution)/shard_map/gather | solution.py:95
  270.8 7.5 %all-to-all-start = ((bf16[32,256,224]{1,2,0:T(8,128)(2,1)}), bf16[32,256,224]{1,2,0:T(8,128)(2,1)}, u32[]{:S(2)}, u32[]{:S(2)}) async-start(bf16[32,256,224]{1,2,0:T(8,128)(2,1)} %copy.33), calls=%async_computation | async-start | bytes 7340032 | tf_op jit(solution)/shard_map/all_to_all | solution.py:98
  278.4 0.2 all-reduce.6.cloned.1.call-start
  278.6 0.1 mul.72
  278.7 46.5 %all-to-all-done = bf16[32,256,224]{1,2,0:T(8,128)(2,1)} async-done(((bf16[32,256,224]{1,2,0:T(8,128)(2,1)}), bf16[32,256,224]{1,2,0:T(8,128)(2,1)}, u32[]{:S(2)}, u32[]{:S(2)}) %all-to-all-start) | async-done | bytes 3670048 | tf_op jit(solution)/shard_map/all_to_all | solution.py:98
  325.2 3.0 fusion.2
  328.2 2.8 fusion.4
  331.0 1.8 copy-done.2
  332.8 0.0 copy-done.3
  332.8 1.1 fusion.9
  334.0 10.1 %fusion.1 = bf16[1,256,7168]{2,1,0:T(8,128)(2,1)} fusion(bf16[1,256,7168]{2,1,0:T(8,128)(2,1)} %param.27, bf16[256,7168]{0,1:T(8,128)(2,1)} %bitcast.76, bf16[1,7168,256]{2,1,0:T(8,128)(2,1)} %param.26, f32[256,256]{1,0:T(8,128)S(1)} %fusion.9), kind=kOutput, calls=%fused_computation.7 | convolution fusion | flops 1881276416 | bytes 14942208 | tf_op jit(solution)/shard_map/dot_general | solution.py:20
  344.0 0.0 all-reduce.6.cloned.1.call-update
  344.0 85.0 %all-reduce.6.cloned.1.call-done = bf16[1,256,7168]{2,1,0:T(8,128)(2,1)} async-done(((bf16[1,256,7168]{2,1,0:T(8,128)(2,1)}), bf16[1,256,7168]{2,1,0:T(8,128)(2,1)}) %all-reduce.6.cloned.1.call-update) | async-done | bytes 3670032 | tf_op jit(solution)/shard_map/psum | solution.py:102
  429.1 15.7 %copy.34 = f32[1,256,7168]{1,0,2:T(1,128)} copy(bf16[1,256,7168]{2,1,0:T(8,128)(2,1)} %all-reduce.6.cloned.1.call-done) | data formatting | bytes 11010048 | tf_op jit(solution)/shard_map/broadcast_in_dim | solution.py:105
  444.8 7.5 %all-to-all-start.1 = ((f32[1,256,7168]{1,0,2:T(1,128)}), f32[1,256,7168]{1,0,2:T(1,128)}, u32[]{:S(2)}, u32[]{:S(2)}) async-start(f32[1,256,7168]{1,0,2:T(1,128)} %copy.34), calls=%async_computation.1 | async-start | bytes 14680064 | tf_op jit(solution)/shard_map/all_to_all | solution.py:105
  452.3 0.1 copy.36
  452.4 113.0 %all-to-all-done.1 = f32[1,256,7168]{1,0,2:T(1,128)} async-done(((f32[1,256,7168]{1,0,2:T(1,128)}), f32[1,256,7168]{1,0,2:T(1,128)}, u32[]{:S(2)}, u32[]{:S(2)}) %all-to-all-start.1) | async-done | bytes 7340064 | tf_op jit(solution)/shard_map/all_to_all | solution.py:105
  565.4 6.6 %copy.38 = f32[1,256,7168]{1,2,0:T(8,128)} copy(f32[1,256,7168]{1,0,2:T(1,128)} %all-to-all-done.1) | data formatting | bytes 14680064
  572.0 8.7 %copy.35 = f32[32,1,256,224]{3,2,0,1:T(8,128)} copy(f32[32,1,256,224]{2,3,0,1:T(8,128)} %bitcast.77) | data formatting | bytes 14680064 | tf_op jit(solution)/shard_map/all_to_all | solution.py:105
  580.6 19.6 %gather_fusion.1 = f32[4096,224]{1,0:T(8,128)} fusion(f32[8192,224]{1,0:T(8,128)} %bitcast.74, s32[4096]{0:T(1024)S(1)} %broadcast_clamp_fusion.1), kind=kCustom, calls=%fused_computation.1 | custom fusion | bytes 7356416 | tf_op jit(solution)/shard_map/gather | solution.py:26
  600.2 4.4 fusion.5
  604.7 0.1 copy.40
  604.8 0.7 fusion.28
  (20 shorter events, 0.1 us)
Async XLA Ops:
  6.5 177.7 %copy-start = (bf16[4096,224]{0,1:T(8,128)(2,1)S(1)}, bf16[4096,224]{0,1:T(8,128)(2,1)}, u32[]{:S(2)}) copy-start(bf16[4096,224]{0,1:T(8,128)(2,1)} %param.20) | copy-start | bytes 5505028
  6.5 177.7 %all-gather.2.cloned.1.call-start = ((), (), s32[]{:S(2)}) async-start(), calls=%async_computation.2 | async-start | bytes 4325376 | tf_op jit(solution)/shard_map/all_gather | solution.py:70
  8.4 6.2 %copy-start.4 = (bf16[16,64,512]{2,1,0:T(8,128)(2,1)S(1)}, bf16[16,64,512]{2,1,0:T(8,128)(2,1)}, u32[]{:S(2)}) copy-start(bf16[16,64,512]{2,1,0:T(8,128)(2,1)} %param.17) | copy-start | bytes 3145732
  20.2 3.8 copy-start.7
  20.2 15.4 %copy-start.10 = (s32[2]{0:T(128)S(1)}, s32[2]{0:T(128)}, u32[]{:S(2)}) copy-start(s32[2]{0:T(128)} %constant.72) | copy-start | bytes 28
  20.3 15.5 %copy-start.9 = (s32[2]{0:T(128)S(1)}, s32[2]{0:T(128)}, u32[]{:S(2)}) copy-start(s32[2]{0:T(128)} %constant.75) | copy-start | bytes 28
  24.0 206.2 %all-reduce.4.cloned.1.call-start = ((), (), s32[]{:S(2)}) async-start(), calls=%async_computation.3 | async-start | bytes 917504 | tf_op jit(solution)/shard_map/psum | solution.py:74
  35.5 194.7 %copy-start.5 = (bf16[512,224]{0,1:T(8,128)(2,1)S(1)}, bf16[512,224]{0,1:T(8,128)(2,1)}, u32[]{:S(2)}) copy-start(bf16[512,224]{0,1:T(8,128)(2,1)} %param.21) | copy-start | bytes 688132
  270.8 7.8 %copy-start.6 = (f32[7168]{0:T(1024)S(1)}, f32[7168]{0:T(1024)}, u32[]{:S(2)}) copy-start(f32[7168]{0:T(1024)} %param.22) | copy-start | bytes 86020
  270.8 54.4 %all-to-all-start = ((bf16[32,256,224]{1,2,0:T(8,128)(2,1)}), bf16[32,256,224]{1,2,0:T(8,128)(2,1)}, u32[]{:S(2)}, u32[]{:S(2)}) async-start(bf16[32,256,224]{1,2,0:T(8,128)(2,1)} %copy.33), calls=%async_computation | async-start | bytes 7340032 | tf_op jit(solution)/shard_map/all_to_all | solution.py:98
  278.4 150.7 %all-reduce.6.cloned.1.call-start = ((), (), s32[]{:S(2)}) async-start(), calls=%async_computation.4 | async-start | bytes 7340032 | tf_op jit(solution)/shard_map/psum | solution.py:102
  328.2 4.6 copy-start.3
  331.0 1.8 copy-start.2
  444.8 7.5 %copy-start.8 = (f32[512,8]{0,1:T(8,128)S(1)}, f32[512,8]{0,1:T(8,128)}, u32[]{:S(2)}) copy-start(f32[512,8]{0,1:T(8,128)} %param.24) | copy-start | bytes 49156
  444.8 120.6 %all-to-all-start.1 = ((f32[1,256,7168]{1,0,2:T(1,128)}), f32[1,256,7168]{1,0,2:T(1,128)}, u32[]{:S(2)}, u32[]{:S(2)}) async-start(f32[1,256,7168]{1,0,2:T(1,128)} %copy.34), calls=%async_computation.1 | async-start | bytes 14680064 | tf_op jit(solution)/shard_map/all_to_all | solution.py:105
  580.6 24.8 %copy-start.1 = (bf16[4096,224]{0,1:T(8,128)(2,1)S(1)}, bf16[4096,224]{0,1:T(8,128)(2,1)}, u32[]{:S(2)}) copy-start(bf16[4096,224]{0,1:T(8,128)(2,1)} %param.20) | copy-start | bytes 5505028
Sparse Core Ops, SparseCore 0:
  24.1 160.0 all-gather.1
  188.8 41.4 all-reduce.3
  344.2 84.8 all-reduce.5
where the time goes:
time: 613 us; the launch traced here: 612 us
  waiting for transfers between devices  419 us (68%)
  local copies, waits for them, and re-layouts  111 us (18%)
  matrix products  30.1 us (5%)
  other arithmetic  23.4 us (4%)
  starting transfers between devices  15.3 us (2%)
  between operations  13.4 us (2%)
    all_gather x1, waiting for transfers between devices, body(): lax.all_gather(head_values, 'dev', axis=0, tiled=True)  148 us
    all_to_all x1, waiting for transfers between devices, body(): lax.all_to_all(summed[None], 'dev', split_axis=2, concat_axis=0, tiled=True)  113 us
    psum x1, waiting for transfers between devices, body(): lax.psum(partial_value.astype(jnp.float32).astype(jnp.bfloat16), 'sec')  85 us
    all_to_all x1, waiting for transfers between devices, body(): lax.all_to_all(outgoing, 'dev', split_axis=0, concat_axis=2, tiled=True)  46.5 us
    gather x2, local copies, waits for them, and re-layouts, body(): outgoing = padded[slot_rows]  39.3 us
    psum x1, waiting for transfers between devices, body(): attn_out = lax.psum(partial_attn, 'sec')  25.9 us
    unnamed x29, local copies, waits for them, and re-layouts  24.4 us
    gather x1, local copies, waits for them, and re-layouts, combine_users(): returned.reshape(-1, columns)[flat_index].reshape(total_rows, topk, columns)  19.6 us
  transfers between devices with their start and end apart: 5, of which 5 were waited for; matrix products, arithmetic and copies ran while one was open for 4% of the time, Pallas kernels for 0%

commit v1 on v0

v1 whole, which is shorter than its diff:
```python
import jax
import jax.numpy as jnp
from jax import lax
from jax.experimental import pallas as pl
from jax.experimental.pallas import tpu as pltpu
from jax.sharding import PartitionSpec as P

ROPE = 64
NOPE = 128
norm_eps = 1e-06
MESH = pl.DeviceIdType.MESH
F32 = jnp.float32
BF16 = jnp.bfloat16

PARTS = ((0, 80, "xyz"), (80, 80, "zxy"), (160, 64, "yzx"))
FEATS = 224
LANES = 128


def gain_planes(norm_gain):
    g = norm_gain.reshape(2, 4, 4, FEATS)
    z_planes = g[..., 0:80].transpose(2, 0, 1, 3).reshape(4, 1, 640)
    y_planes = g[..., 80:160].transpose(1, 0, 2, 3).reshape(4, 1, 640)
    x_planes = g[..., 160:224].reshape(2, 1, 1024)
    return z_planes, y_planes, x_planes


def weight_plane(ref, p, j):
    first, rows, _ = PARTS[p]
    if p == 0:
        block = ref[:, :, j, first : first + rows, :]
    elif p == 1:
        block = ref[:, j, :, first : first + rows, :]
    else:
        block = ref[j, :, :, first : first + rows, :]
    return block.reshape(-1, block.shape[-1])


def at(ref, **index):
    return ref.at[tuple(index.get(axis, slice(None)) for axis in "xyz")]


def get(ref, **index):
    return ref[tuple(index.get(axis, slice(None)) for axis in "xyz")]


def moe_kernel(
    head_hbm, out_proj_hbm, hidden_hbm, gain0, gain1, gain2, share_ref, gate_hbm, up_hbm, down_hbm,
    out_ref,
    heads0, heads1, out_proj, attn, pair_in, far_in, far_out, hidden,
    gate_in, up_in, down_in, wt0, wt1, wt2, downt,
    rt0, rt1, rt2, gate_up, act, o0, o1, o2,
    r1_0, r1_1, r1_2, r2_0, r2_1, r2_2, r3_0, r3_1, r3_2, r4_0, r4_1, r4_2, r5_0, r5_1, r5_2,
    local_sem, send_sem, recv_sem,
):
    sec = lax.axis_index("sec")
    dev = lax.axis_index("dev")
    x_hi, core = sec // 2, lax.rem(sec, 2)
    x_lo = dev // 16
    me = {
        "x": x_hi * 2 + x_lo,
        "y": lax.rem(dev // 4, 4),
        "z": lax.rem(dev, 4),
    }

    def shift(axis, by):
        return lax.rem(me[axis] + (by % 4), 4)

    def device(x, y, z, c):
        return ((x // 2) * 2 + c, lax.rem(x, 2) * 16 + y * 4 + z)

    def neighbour(axis, by):
        place = dict(me)
        place[axis] = shift(axis, by)
        return device(place["x"], place["y"], place["z"], core)

    partner = device(me["x"], me["y"], me["z"], 1 - core)
    x_lo_partner = (sec, (1 - x_lo) * 16 + me["y"] * 4 + me["z"])

    tags = {}
    sent = []

    def number(tag):
        return tags.setdefault(tag, len(tags))

    def send(tag, src, dst, to):
        i = number(tag)
        copy = pltpu.make_async_remote_copy(
            src_ref=src, dst_ref=dst, send_sem=send_sem.at[i], recv_sem=recv_sem.at[i],
            device_id=to, device_id_type=MESH,
        )
        copy.start()
        sent.append(copy)

    def recv(tag, region):
        i = number(tag)
        pltpu.make_async_remote_copy(
            src_ref=region, dst_ref=region, send_sem=send_sem.at[i], recv_sem=recv_sem.at[i],
            device_id=partner, device_id_type=MESH,
        ).wait_recv()

    heads = (heads0, heads1)
    own_heads = [at(h, x=x_lo, y=me["y"], z=me["z"]) for h in heads]
    my_hidden = hidden_hbm.at[pl.ds(pl.multiple_of(sec * LANES, LANES), LANES)]
    loads = [
        pltpu.make_async_copy(head_hbm.at[0], own_heads[0], local_sem.at[0]),
        pltpu.make_async_copy(head_hbm.at[1], own_heads[1], local_sem.at[1]),
        pltpu.make_async_copy(gate_hbm, gate_in, local_sem.at[2]),
        pltpu.make_async_copy(up_hbm, up_in, local_sem.at[3]),
        pltpu.make_async_copy(out_proj_hbm, out_proj, local_sem.at[4]),
        pltpu.make_async_copy(down_hbm, down_in, local_sem.at[5]),
        pltpu.make_async_copy(my_hidden, hidden, local_sem.at[6]),
    ]
    for load in loads:
        load.start()

    barrier = pltpu.get_barrier_semaphore()
    around = [neighbour(axis, by) for axis in "xyz" for by in (1, 2, 3)] + [partner]
    for other in around:
        pl.semaphore_signal(barrier, inc=1, device_id=other, device_id_type=MESH)
    pl.semaphore_wait(barrier, len(around))

    order = (("y", "z"), ("z", "y"))
    half = heads0.shape[-1]

    def head_block(p, k, **index):
        place = {"x": lax.rem(x_lo + k, 2), "y": me["y"], "z": me["z"]}
        place.update(index)
        return at(heads[p], **place)

    def head_slab(p, **index):
        return at(heads[p], **index)

    for p in range(2):
        loads[p].wait()
        send(("hx", p), own_heads[p], own_heads[p], x_lo_partner)
    for p in range(2):
        b, c = order[p]
        for by in (1, 3):
            send(("hb", p, 0, by), own_heads[p], own_heads[p], neighbour(b, by))

    wts = (wt0, wt1, wt2)
    gains = (gain0, gain1, gain2)

    def transpose_part(p, which):
        source = (gate_in, up_in)[which]

        def step(j, carry):
            block = weight_plane(source, p, j).T.astype(F32) * gains[p][j]
            wts[p][0, j, which * 256 : which * 256 + 256, :] = block.astype(BF16)
            return carry

        lax.fori_loop(0, wts[p].shape[1], step, 0)

    def transpose_down():
        def step(j, carry):
            block = down_in[:, pl.ds(pl.multiple_of(j * 896, 896), 896)].T
            downt[0, j // 4, lax.rem(j, 4)] = block.reshape(4, FEATS, 256)
            return carry

        lax.fori_loop(0, 8, step, 0)

    def share_part(p):
        send(("wt", p), wts[p].at[0], wts[p].at[1], partner)

    def task_first():
        loads[2].wait()
        loads[3].wait()
        transpose_part(0, 0)

    def task_1():
        transpose_part(0, 1)
        share_part(0)

    def task_2():
        transpose_part(1, 0)

    def task_3():
        transpose_part(1, 1)
        share_part(1)

    def task_4():
        transpose_part(2, 0)

    def task_5():
        transpose_part(2, 1)
        share_part(2)

    def task_6():
        loads[5].wait()
        transpose_down()
        send(("dn",), downt.at[0], downt.at[1], partner)

    tasks = [task_first, task_1, task_2, task_3, task_4, task_5, task_6]

    def work():
        if tasks:
            tasks.pop(0)()

    work()

    def slab_sends(p, m):
        b, c = order[p]
        slab = head_slab(p, **{b: shift(b, m), c: me[c]})
        for by in (1, 3):
            send(("hc", p, m, by), slab, slab, neighbour(c, by))

    for p in range(2):
        b, c = order[p]
        other = head_block(p, 1)
        recv(("hx", p), other)
        for by in (1, 3):
            send(("hb", p, 1, by), other, other, neighbour(b, by))
    for p in range(2):
        slab_sends(p, 0)
    work()
    for p in range(2):
        b, c = order[p]
        block = head_block(p, 0, **{b: shift(b, 3)})
        recv(("hb", p, 0, 1), block)
        send(("hf", p, 0), block, block, neighbour(b, 1))
        recv(("hb", p, 0, 3), head_block(p, 0, **{b: shift(b, 1)}))
    for p in range(2):
        b, c = order[p]
        block = head_block(p, 1, **{b: shift(b, 1)})
        recv(("hb", p, 1, 3), block)
        send(("hf", p, 1), block, block, neighbour(b, 3))
        slab_sends(p, 1)
        recv(("hb", p, 1, 1), head_block(p, 1, **{b: shift(b, 3)}))
        slab_sends(p, 3)
    work()
    for p in range(2):
        b, c = order[p]
        for k in range(2):
            recv(("hf", p, k), head_block(p, k, **{b: shift(b, 2)}))
        slab_sends(p, 2)
    work()

    def project(p, by, first=False):
        c = order[p][1]
        j = shift(c, by)
        rows = get(heads[p], **{c: j}).reshape(-1, half)
        product = jnp.dot(rows, out_proj[p * half : (p + 1) * half, :], preferred_element_type=F32)
        product = product.reshape(2, 4, 16, FEATS)
        if c == "z":
            attn[:, :, j] = product
        else:
            attn[:, j] += product

    loads[4].wait()
    project(0, 0)
    for m in (0, 1, 3, 2):
        for p in range(2):
            b, c = order[p]
            for by in (1, 3):
                region = head_slab(p, **{b: shift(b, m), c: shift(c, -by)})
                recv(("hc", p, m, by), region)
                if (m in (0, 1)) == (by == 1):
                    send(("hd", p, m), region, region, neighbour(c, by))
        work()
    while tasks:
        work()
    project(0, 1)
    project(0, 3)
    for m in (0, 3, 1, 2):
        for p in range(2):
            b, c = order[p]
            recv(("hd", p, m), head_slab(p, **{b: shift(b, m), c: shift(c, 2)}))
    project(0, 2)
    for by in (0, 1, 3, 2):
        project(1, by)

    attn_mine = attn.at[:, pl.ds(core * 2, 2)]
    send(("pair",), attn.at[:, pl.ds((1 - core) * 2, 2)], pair_in, partner)
    recv(("pair",), pair_in)
    far_out[...] = (attn_mine[1 - x_hi] + pair_in[1 - x_hi]).astype(BF16)
    send(("far",), far_out, far_in, neighbour("x", 2))
    loads[6].wait()
    near = (attn_mine[x_hi] + pair_in[x_hi]).reshape(LANES, FEATS) + hidden[...].astype(F32)
    recv(("far",), far_in)
    residual = near + far_in[...].reshape(LANES, FEATS).astype(F32)
    residual = jnp.concatenate([residual, jnp.zeros((LANES, 32), F32)], axis=1).T[:FEATS]
    out_ref[...] = residual
    routed = residual.astype(BF16)

    rts = (rt0, rt1, rt2)
    for p, (first, rows, _) in enumerate(PARTS):
        rts[p][me["x"], me["y"], me["z"]] = routed[first : first + rows]

    def spot(p, **index):
        place = dict(me)
        place.update(index)
        return at(rts[p], **place)

    axes = [tuple(o) for _, _, o in PARTS]
    for p in range(3):
        a, b, c = axes[p]
        for by in (1, 3, 2):
            send(("ga", p, by), spot(p), spot(p), neighbour(a, by))
        for by in (1, 3):
            send(("gb", p, 0, by), spot(p), spot(p), neighbour(b, by))

    def plane_group(p, m):
        a, b, c = axes[p]
        slab = at(rts[p], **{b: shift(b, m), c: me[c]})
        for by in (1, 3):
            send(("gc", p, m, by), slab, slab, neighbour(c, by))

    for k in (1, 3, 2):
        for p in range(3):
            a, b, c = axes[p]
            block = spot(p, **{a: shift(a, k)})
            recv(("ga", p, 4 - k), block)
            for by in (1, 3):
                send(("gb", p, k, by), block, block, neighbour(b, by))
    for p in range(3):
        plane_group(p, 0)
    for k in (0, 1, 3, 2):
        for p in range(3):
            a, b, c = axes[p]
            for by in (1, 3):
                block = spot(p, **{a: shift(a, k), b: shift(b, -by)})
                recv(("gb", p, k, by), block)
                if (k in (0, 1)) == (by == 1):
                    send(("gf", p, k), block, block, neighbour(b, by))
    for p in range(3):
        plane_group(p, 3)
        plane_group(p, 1)
    for p in range(3):
        a, b, c = axes[p]
        for k in (0, 1, 3, 2):
            recv(("gf", p, k), spot(p, **{a: shift(a, k), b: shift(b, 2)}))
        plane_group(p, 2)

    for p in range(3):
        recv(("wt", p), wts[p].at[1])
    totals = {"square": jnp.zeros((1, 256), F32), "first": True}

    def users_of(p, by):
        if p == 0:
            block = rts[0][:, :, shift("z", by)]
            low, high = block[0:2], block[2:4]
        elif p == 1:
            block = rts[1][:, shift("y", by)]
            low, high = block[0:2], block[2:4]
        else:
            plane = lax.rem(x_lo + by, 2)
            low, high = rts[2][plane], rts[2][plane + 2]
        return jnp.concatenate([low.reshape(-1, LANES), high.reshape(-1, LANES)], axis=1)

    def plane_of(p, by):
        if p == 2:
            return lax.rem(x_lo + by, 2)
        return shift(axes[p][2], by)

    def multiply(p, by):
        rows = users_of(p, by)
        wide = rows.astype(F32)
        totals["square"] = totals["square"] + jnp.sum(wide * wide, axis=0, keepdims=True)
        for slot in range(2):
            product = jnp.dot(wts[p][slot, plane_of(p, by)], rows, preferred_element_type=F32)
            if totals["first"]:
                gate_up[slot] = product
            else:
                gate_up[slot] += product
        totals["first"] = False

    multiply(0, 0)
    multiply(1, 0)
    for m in (0, 1, 3, 2):
        for p in range(3):
            a, b, c = axes[p]
            for by in (1, 3):
                region = at(rts[p], **{b: shift(b, m), c: shift(c, -by)})
                recv(("gc", p, m, by), region)
                if (m in (0, 1)) == (by == 1):
                    send(("gd", p, m), region, region, neighbour(c, by))
    for by in (1, 3):
        multiply(0, by)
        multiply(1, by)
    multiply(2, 1)
    for p in range(3):
        a, b, c = axes[p]
        for m in (0, 3, 1, 2):
            recv(("gd", p, m), at(rts[p], **{b: shift(b, m), c: shift(c, 2)}))
        multiply(p, 2 if p < 2 else 0)

    scale = lax.rsqrt(totals["square"] * (1.0 / (32 * FEATS)) + norm_eps)
    for slot in range(2):
        gate = gate_up[slot, 0:256] * scale
        upward = gate_up[slot, 256:512] * scale
        act[slot * 256 : slot * 256 + 256] = (gate / (1.0 + jnp.exp(-gate)) * upward).astype(BF16)

    recv(("dn",), downt.at[1])
    outs = (o0, o1, o2)
    r1, r2, r3, r4, r5 = (
        (r1_0, r1_1, r1_2), (r2_0, r2_1, r2_2), (r3_0, r3_1, r3_2), (r4_0, r4_1, r4_2), (r5_0, r5_1, r5_2)
    )
    share = jnp.concatenate([share_ref[core], share_ref[core + 2]], axis=1)

    def down(p, by):
        first, rows, _ = PARTS[p]
        j = plane_of(p, by)
        product = jnp.dot(weight_plane(downt.at[0], p, j), act[0:256], preferred_element_type=F32)
        product += jnp.dot(weight_plane(downt.at[1], p, j), act[256:512], preferred_element_type=F32)
        product = (product * share).astype(BF16)
        for h in range(2):
            lanes = product[:, h * LANES : (h + 1) * LANES]
            if p == 0:
                o0[2 * h : 2 * h + 2, :, j] = lanes.reshape(2, 4, rows, LANES)
            elif p == 1:
                o1[2 * h : 2 * h + 2, j] = lanes.reshape(2, 4, rows, LANES)
            else:
                o2[j + 2 * h] = lanes.reshape(4, 4, rows, LANES)

    def o_slab(p, by, m):
        a, b, c = axes[p]
        return at(outs[p], **{c: shift(c, by), b: shift(b, m)})

    for p in range(3):
        c = axes[p][2]
        down(p, 2 if p < 2 else 0)
        for m in (2, 0, 3, 1):
            by = 1 if m in (0, 1) else 3
            send(("s1", p, m), o_slab(p, 2, m), r1[p].at[m], neighbour(c, by))
    for p in range(3):
        c = axes[p][2]
        if p < 2:
            down(p, 1)
            down(p, 3)
        else:
            down(p, 1)
        for m in (2, 3):
            send(("s2", p, 0, m), o_slab(p, 1, m), r2[p].at[0, m], neighbour(c, 1))
        for m in (1, 0):
            send(("s2", p, 1, m), o_slab(p, 3, m), r2[p].at[1, m], neighbour(c, 3))
    for p in range(2):
        down(p, 0)

    def add_to(slab, other):
        slab[...] = (slab[...].astype(F32) + other[...].astype(F32)).astype(BF16)

    for m in (2, 1, 3, 0):
        for p in range(3):
            c = axes[p][2]
            recv(("s1", p, m), r1[p].at[m])
            by = 1 if m in (0, 1) else 3
            side = 0 if by == 1 else 1
            slab = o_slab(p, by, m)
            add_to(slab, r1[p].at[m])
            send(("s2", p, side, m), slab, r2[p].at[side, m], neighbour(c, by))

    for m in (2, 1, 3, 0):
        for p in range(3):
            a, b, c = axes[p]
            slab = o_slab(p, 0, m)
            for side in range(2):
                recv(("s2", p, side, m), r2[p].at[side, m])
            slab[...] = (
                slab[...].astype(F32) + r2[p][0, m].astype(F32) + r2[p][1, m].astype(F32)
            ).astype(BF16)
            if m == 2:
                send(("s3", p, 0), slab.at[0:2], r3[p].at[0:2], neighbour(b, 1))
                send(("s3", p, 1), slab.at[2:4], r3[p].at[2:4], neighbour(b, 3))
            elif m == 1:
                send(("s4", p, 0, 1), slab.at[2:4], r4[p].at[0, 2:4], neighbour(b, 1))
            elif m == 3:
                send(("s4", p, 1, 0), slab.at[0:2], r4[p].at[1, 0:2], neighbour(b, 3))
    for p in range(3):
        a, b, c = axes[p]
        recv(("s3", p, 0), r3[p].at[0:2])
        slab = o_slab(p, 0, 1).at[0:2]
        add_to(slab, r3[p].at[0:2])
        send(("s4", p, 0, 0), slab, r4[p].at[0, 0:2], neighbour(b, 1))
        recv(("s3", p, 1), r3[p].at[2:4])
        slab = o_slab(p, 0, 3).at[2:4]
        add_to(slab, r3[p].at[2:4])
        send(("s4", p, 1, 1), slab, r4[p].at[1, 2:4], neighbour(b, 3))
    for p in range(3):
        a, b, c = axes[p]
        for side in range(2):
            for lower in range(2):
                recv(("s4", p, side, lower), r4[p].at[side, 2 * lower : 2 * lower + 2])
        slab = o_slab(p, 0, 0)
        slab[...] = (
            slab[...].astype(F32) + r4[p][0].astype(F32) + r4[p][1].astype(F32)
        ).astype(BF16)
        for k in (2, 1, 3):
            send(("s5", p, k), slab.at[shift(a, k)], r5[p].at[k - 1], neighbour(a, k))
    for p, (first, rows, _) in enumerate(PARTS):
        a = axes[p][0]
        total = out_ref[first : first + rows, :] + outs[p][me["x"], me["y"], me["z"]].astype(F32)
        for k in (1, 3, 2):
            recv(("s5", p, k), r5[p].at[k - 1])
            total = total + r5[p][k - 1].astype(F32)
        out_ref[first : first + rows, :] = total
    for copy in sent:
        copy.wait_send()
    print("messages", len(tags))


def remote_part(head_values, output_proj, hidden, gains, share, gate, up, down):
    def bf(*shape):
        return pltpu.VMEM(shape, BF16)

    def f32(*shape):
        return pltpu.VMEM(shape, F32)

    rows = [r for _, r, _ in PARTS]
    any_space = pl.BlockSpec(memory_space=pl.ANY)
    vmem = pl.BlockSpec(memory_space=pltpu.VMEM)
    half = head_values.shape[-1]
    scratch = [
        bf(2, 4, 4, 16, half), bf(2, 4, 4, 16, half), bf(*output_proj.shape), f32(2, 4, 4, 16, FEATS),
        f32(2, 2, 4, 16, FEATS), bf(2, 4, 16, FEATS), bf(2, 4, 16, FEATS), bf(LANES, FEATS),
        bf(2, 4, 4, FEATS, 256), bf(2, 4, 4, FEATS, 256), bf(256, 32 * FEATS),
        bf(2, 4, 512, 640), bf(2, 4, 512, 640), bf(2, 2, 512, 1024), bf(2, 2, 4, 4, FEATS, 256),
        *[bf(4, 4, 4, r, LANES) for r in rows],
        f32(2, 512, 256), bf(512, 256),
        *[bf(4, 4, 4, r, LANES) for r in rows],
        *[bf(4, 4, r, LANES) for r in rows],
        *[bf(2, 4, 4, r, LANES) for r in rows],
        *[bf(4, r, LANES) for r in rows],
        *[bf(2, 4, r, LANES) for r in rows],
        *[bf(3, r, LANES) for r in rows],
        pltpu.SemaphoreType.DMA((7,)),
        pltpu.SemaphoreType.DMA((256,)),
        pltpu.SemaphoreType.DMA((256,)),
    ]
    return pl.pallas_call(
        moe_kernel,
        out_shape=jax.ShapeDtypeStruct((FEATS, LANES), F32),
        in_specs=[any_space, any_space, any_space, vmem, vmem, vmem, vmem, any_space, any_space, any_space],
        out_specs=vmem,
        scratch_shapes=scratch,
        compiler_params=pltpu.CompilerParams(
            collective_id=0, has_side_effects=True, vmem_limit_bytes=60 * 1024 * 1024
        ),
        cost_estimate=pl.CostEstimate(flops=7 * 10**9, bytes_accessed=16 * 2**20, transcendentals=0),
    )(head_values, output_proj, hidden, *gains, share, gate, up, down)


def body(
    query_latent, query_rope, cache_latent, cache_rope, lengths, value_up, output_proj, hidden,
    norm_gain, route_ids, route_weights, gate_proj, up_proj, down_proj,
):
    users_here, heads_here, latent_width = query_latent.shape
    history = cache_latent.shape[1]
    rope_width = cache_rope.shape[1]
    positional = query_rope.reshape(users_here, heads_here, rope_width)
    scores = jnp.einsum(
        "rhc,rtc->rht", query_latent, cache_latent, preferred_element_type=jnp.float32
    )
    scores = scores + jnp.einsum(
        "rhe,ret->rht", positional, cache_rope, preferred_element_type=jnp.float32
    )
    scores = scores * (NOPE + ROPE) ** (-0.5)
    visible = jnp.arange(history, dtype=jnp.int32)[None, None, :] < lengths[:, None, None]
    scores = jnp.where(visible, scores, -1e30)
    highest = jnp.max(scores, axis=-1, keepdims=True)
    exponent = jnp.exp(scores - highest)
    attn_weights = (exponent / jnp.sum(exponent, axis=-1, keepdims=True)).astype(jnp.bfloat16)
    context = jnp.einsum(
        "rht,rtc->rhc", attn_weights, cache_latent, preferred_element_type=jnp.float32
    ).astype(jnp.bfloat16)
    head_values = jnp.einsum(
        "rhc,hcv->rhv", context, value_up, preferred_element_type=jnp.float32
    ).astype(jnp.bfloat16)
    head_values = head_values.reshape(users_here, 2, -1).transpose(1, 0, 2)

    expert = lax.axis_index("dev")
    share = jnp.sum(jnp.where(route_ids == expert, route_weights, 0.0), axis=1).reshape(4, 1, LANES)
    out = remote_part(
        head_values, output_proj, hidden, gain_planes(norm_gain), share,
        gate_proj.reshape(2, 4, 4, FEATS, 256), up_proj.reshape(2, 4, 4, FEATS, 256), down_proj[0],
    )
    return out.T.astype(BF16)


def solution(mesh):
    return jax.shard_map(
        body,
        mesh=mesh,
        in_specs=(
            P("dev", "sec", None),
            P("dev", "sec"),
            P("dev", None, None),
            P("dev", None, None),
            P("dev"),
            P("sec", None, None),
            P("sec", "dev"),
            P(None, "dev"),
            P(),
            P(),
            P(),
            P("dev", None, "sec"),
            P("dev", None, "sec"),
            P("dev", "sec", None),
        ),
        out_specs=P("sec", "dev"),
        check_vma=False,
    )
```

time: 613 us -> 119 us (0.19)
  waiting for transfers between devices: 419 us -> 0 us
  local copies, waits for them, and re-layouts: 111 us -> 9.17 us
  Pallas kernels: 0 us -> 90.9 us
  other arithmetic: 23.4 us -> 3.97 us
  matrix products: 30.1 us -> 14.6 us
  starting transfers between devices: 15.3 us -> 0 us
  between operations: 13.4 us -> 0.07 us
    all_to_all x2 -> x0, waiting for transfers between devices: 159 us -> none  [the longest x1 113 us: body(): lax.all_to_all(summed[None], 'dev', split_axis=2, concat_axis=0, tiled=True)]
    all_gather x1 -> x0, waiting for transfers between devices: 148 us -> none  [body(): lax.all_gather(head_values, 'dev', axis=0, tiled=True)]
    psum x2 -> x0, waiting for transfers between devices: 111 us -> none  [the longest x1 85 us: body(): lax.psum(partial_value.astype(jnp.float32).astype(jnp.bfloat16), 'sec')]
    pallas_call x0 -> x1, Pallas kernels: none -> 90.9 us  [remote_part(): pl.pallas_call(moe_kernel, out_shape=jax.ShapeDtypeStruct((FEATS, LANES),...]
    gather x3 -> x0, local copies, waits for them, and re-layouts: 58.9 us -> none  [the longest x2 39.3 us: body(): outgoing = padded[slot_rows]]
    unnamed x29 -> x6, local copies, waits for them, and re-layouts: 24.4 us -> 4.31 us
    broadcast_in_dim x1 -> x0, local copies, waits for them, and re-layouts: 15.7 us -> none  [body(): summed[None]]
    dot_general x3 -> x0, matrix products: 15.6 us -> none  [the longest x1 10.1 us: expert_partial(): jnp.dot(activation, down_w, preferred_element_type=jnp.float32)]
  transfers between devices with their start and end apart: 5 -> 0, of which waited for: 5 -> 0; matrix products, arithmetic and copies ran while one was open for 4% -> 0% of each run, Pallas kernels for 0% -> 0%
where the time goes in v1:
time: 119 us
  Pallas kernels  90.9 us (76%)
  matrix products  14.6 us (12%)
  local copies, waits for them, and re-layouts  9.17 us (8%)
  other arithmetic  3.97 us (3%)
    pallas_call x1, Pallas kernels, remote_part(): pl.pallas_call(moe_kernel, out_shape=jax.ShapeDtypeStruct((FEATS, LANES),...  90.9 us
    dot_general x1, matrix products, body(): jnp.einsum('rhc,rtc->rht', query_latent, cache_latent, preferred_element_...  6.09 us
    dot_general x1, matrix products, body(): jnp.einsum('rht,rtc->rhc', attn_weights, cache_latent, preferred_element_...  4.97 us
    unnamed x6, local copies, waits for them, and re-layouts  4.31 us
    dot_general x1, matrix products, body(): jnp.einsum('rhc,hcv->rhv', context, value_up, preferred_element_type=jnp....  3.17 us

profile of v1, /device:TPU:0, one launch (start us, length us, event | category | flops | bytes accessed | tf_op | source)
XLA Modules:
  0.0 118.7 jit_solution(14780037424928872772)
XLA Ops:
  0.0 0.0 copy-start
  0.0 1.4 %select_reduce_fusion = f32[512]{0:T(512)} fusion(f32[512,8]{0,1:T(8,128)} %param.24, s32[512,8]{0,1:T(8,128)} %param.23, s32[]{:T(128)S(6)} %axis_index.12), kind=kLoop, calls=%fused_computation.17 | loop fusion | flops 11776 | bytes 34820 | tf_op jit(solution)/shard_map/reduce_sum | solution.py:572
  1.4 0.7 iota_compare_fusion
  2.1 0.8 reshape.52
  3.0 0.1 slice.14
  3.1 0.7 reshape.55.gain2
  3.7 0.1 slice_bitcast_fusion
  3.8 0.7 reshape.54.gain1
  4.5 0.7 reshape.53.gain0
  5.2 1.0 reshape.50
  6.3 1.8 %copy.24.hidden_hbm = bf16[512,224]{1,0:T(8,128)(2,1)} copy(bf16[512,224]{0,1:T(8,128)(2,1)} %param.21) | data formatting | bytes 458752 | tf_op args[7]
  8.1 6.1 %fusion.10 = f32[16,32,512]{2,1,0:T(8,128)S(1)} fusion(bf16[16,32,512]{2,1,0:T(8,128)(2,1)} %param.14, bf16[16,512,512]{2,1,0:T(8,128)(2,1)} %param.16), kind=kOutput, calls=%fused_computation.20 | convolution fusion | flops 268435456 | bytes 9961472 | tf_op jit(solution)/shard_map/rhc,rtc->rht/dot_general | solution.py:551
  14.2 0.0 copy-done
  14.2 0.3 fusion.4
  14.5 0.3 fusion.9
  14.8 5.0 %fusion.6 = bf16[16,32,512]{2,1,0:T(8,128)(2,1)S(1)} fusion(bf16[16,512,512]{2,1,0:T(8,128)(2,1)} %param.16, f32[16,32]{1,0:T(8,128)S(1)} %fusion.9, f32[16,32,512]{2,1,0:T(8,128)S(1)} %fusion.4), kind=kOutput, calls=%fused_computation.10 | convolution fusion | flops 269222912 | bytes 9963520 | tf_op jit(solution)/shard_map/rht,rtc->rhc/dot_general | solution.py:563
  19.8 0.0 copy-start.1
  19.8 3.2 %fusion.5 = bf16[16,32,128]{2,0,1:T(8,128)(2,1)S(1)} fusion(bf16[32,512,128]{2,1,0:T(8,128)(2,1)} %param.19, bf16[16,32,512]{2,1,0:T(8,128)(2,1)S(1)} %fusion.6), kind=kOutput, calls=%fused_computation.7 | convolution fusion | flops 67174400 | bytes 4849664 | tf_op jit(solution)/shard_map/rhc,hcv->rhv/dot_general | solution.py:566
  23.1 0.7 copy.29
  23.7 0.0 copy-done.1
  23.7 2.5 %copy.23.out_proj_hbm = bf16[4096,224]{1,0:T(8,128)(2,1)} copy(bf16[4096,224]{0,1:T(8,128)(2,1)S(1)} %copy-done.1) | data formatting | bytes 3670016 | tf_op args[6]
  26.2 90.9 %shard_map.136 = f32[224,128]{1,0:T(8,128)} custom-call(bf16[2,16,2048]{2,1,0:T(8,128)(2,1)} %bitcast.23, bf16[4096,224]{1,0:T(8,128)(2,1)} %copy.23.out_proj_hbm, bf16[512,224]{1,0:T(8,128)(2,1)} %copy.24.hidden_hbm, f32[4,1,640]{2,1,0:T(1,128)} %reshape.53.gain0, f32[4,1,640]{2,1,0:T(1,128)} %reshape.54.gain1, f32[2,1,1024]{2,1,0:T(1,128)} %reshape.55.gain2, ...), custom_call_target="tpu_custom_call" | custom-call | flops 7000000000 | bytes 16777216 | tf_op jit(solution)/shard_map/pallas_call | solution.py:530
  117.2 1.5 %convert_bitcast_fusion = bf16[128,224]{0,1:T(8,128)(2,1)} fusion(f32[224,128]{1,0:T(8,128)} %shard_map.136), kind=kLoop, calls=%fused_computation.13 | loop fusion | flops 28672 | bytes 172032 | tf_op jit(solution)/shard_map/convert_element_type | solution.py:577
  (4 shorter events, 0.1 us)
Async XLA Ops:
  0.0 14.2 %copy-start = (bf16[16,64,512]{2,1,0:T(8,128)(2,1)S(1)}, bf16[16,64,512]{2,1,0:T(8,128)(2,1)}, u32[]{:S(2)}) copy-start(bf16[16,64,512]{2,1,0:T(8,128)(2,1)} %param.17) | copy-start | bytes 3145732
  19.8 4.0 %copy-start.1 = (bf16[4096,224]{0,1:T(8,128)(2,1)S(1)}, bf16[4096,224]{0,1:T(8,128)(2,1)}, u32[]{:S(2)}) copy-start(bf16[4096,224]{0,1:T(8,128)(2,1)} %param.20) | copy-start | bytes 5505028

commit v2 on v1

--- a/solution.py
+++ b/solution.py
@@ -1,3 +1,5 @@
+import functools
+
 import jax
 import jax.numpy as jnp
 from jax import lax
@@ -15,14 +17,7 @@
 PARTS = ((0, 80, "xyz"), (80, 80, "zxy"), (160, 64, "yzx"))
 FEATS = 224
 LANES = 128
-
-
-def gain_planes(norm_gain):
-    g = norm_gain.reshape(2, 4, 4, FEATS)
-    z_planes = g[..., 0:80].transpose(2, 0, 1, 3).reshape(4, 1, 640)
-    y_planes = g[..., 80:160].transpose(1, 0, 2, 3).reshape(4, 1, 640)
-    x_planes = g[..., 160:224].reshape(2, 1, 1024)
-    return z_planes, y_planes, x_planes
+GROUP = 4
 
 
 def weight_plane(ref, p, j):
@@ -44,14 +39,16 @@
     return ref[tuple(index.get(axis, slice(None)) for axis in "xyz")]
 
 
-def moe_kernel(
-    head_hbm, out_proj_hbm, hidden_hbm, gain0, gain1, gain2, share_ref, gate_hbm, up_hbm, down_hbm,
+def layer_kernel(
+    query_hbm, rope_hbm, cache_hbm, keys_hbm, lengths_ref, value_up_hbm,
+    out_proj_hbm, hidden_hbm, gain_ref, ids_ref, weights_ref, gate_hbm, up_hbm, down_hbm,
     out_ref,
+    query, rope, positional, cache, keys, context, value_up,
     heads0, heads1, out_proj, attn, pair_in, far_in, far_out, hidden,
-    gate_in, up_in, down_in, wt0, wt1, wt2, downt,
+    weight_in, down_in, gain0, gain1, gain2, wt0, wt1, wt2, downt,
     rt0, rt1, rt2, gate_up, act, o0, o1, o2,
     r1_0, r1_1, r1_2, r2_0, r2_1, r2_2, r3_0, r3_1, r3_2, r4_0, r4_1, r4_2, r5_0, r5_1, r5_2,
-    local_sem, send_sem, recv_sem,
+    cache_sem, local_sem, send_sem, recv_sem,
 ):
     sec = lax.axis_index("sec")
     dev = lax.axis_index("dev")
@@ -99,29 +96,115 @@
             device_id=partner, device_id_type=MESH,
         ).wait_recv()
 
+    around = [neighbour(axis, by) for axis in "xyz" for by in (1, 2, 3)] + [partner]
+    barrier = pltpu.get_barrier_semaphore()
+    for other in around:
+        pl.semaphore_signal(barrier, inc=1, device_id=other, device_id_type=MESH)
+
     heads = (heads0, heads1)
+    half = heads0.shape[-1]
     own_heads = [at(h, x=x_lo, y=me["y"], z=me["z"]) for h in heads]
-    my_hidden = hidden_hbm.at[pl.ds(pl.multiple_of(sec * LANES, LANES), LANES)]
+    my_hidden = hidden_hbm.at[:, pl.ds(pl.multiple_of(sec * LANES, LANES), LANES)]
+
+    def user_loads(step):
+        slot = lax.rem(step, 2) if not isinstance(step, int) else step % 2
+        users, place = pl.ds(step * GROUP, GROUP), pl.ds(slot * GROUP, GROUP)
+        return (
+            pltpu.make_async_copy(cache_hbm.at[users], cache.at[place], cache_sem.at[slot, 0]),
+            pltpu.make_async_copy(keys_hbm.at[users], keys.at[place], cache_sem.at[slot, 1]),
+        )
+
     loads = [
-        pltpu.make_async_copy(head_hbm.at[0], own_heads[0], local_sem.at[0]),
-        pltpu.make_async_copy(head_hbm.at[1], own_heads[1], local_sem.at[1]),
-        pltpu.make_async_copy(gate_hbm, gate_in, local_sem.at[2]),
-        pltpu.make_async_copy(up_hbm, up_in, local_sem.at[3]),
+        pltpu.make_async_copy(rope_hbm, rope, local_sem.at[0]),
+        pltpu.make_async_copy(query_hbm, query, local_sem.at[1]),
+        pltpu.make_async_copy(value_up_hbm, value_up, local_sem.at[2]),
+        pltpu.make_async_copy(gate_hbm, weight_in, local_sem.at[3]),
         pltpu.make_async_copy(out_proj_hbm, out_proj, local_sem.at[4]),
         pltpu.make_async_copy(down_hbm, down_in, local_sem.at[5]),
         pltpu.make_async_copy(my_hidden, hidden, local_sem.at[6]),
+        pltpu.make_async_copy(up_hbm, weight_in, local_sem.at[7]),
     ]
-    for load in loads:
-        load.start()
-
-    barrier = pltpu.get_barrier_semaphore()
-    around = [neighbour(axis, by) for axis in "xyz" for by in (1, 2, 3)] + [partner]
-    for other in around:
-        pl.semaphore_signal(barrier, inc=1, device_id=other, device_id_type=MESH)
-    pl.semaphore_wait(barrier, len(around))
+    for copy in (loads[0], loads[1], *user_loads(0), *user_loads(1)):
+        copy.start()
+    for n in (2, 3, 4, 5, 6):
+        loads[n].start()
+
+    for p, gain in enumerate((gain0, gain1, gain2)):
+        first, rows, _ = PARTS[p]
+        width = gain.shape[-1]
+        column = lax.broadcasted_iota(jnp.int32, (rows, width), 1)
+        spread = (lax.rem(column, rows) == lax.broadcasted_iota(jnp.int32, (rows, width), 0)).astype(F32)
+        spread = jnp.dot(
+            gain_ref[:, first : first + rows], spread,
+            preferred_element_type=F32, precision=lax.Precision.HIGHEST,
+        )
+        block = lax.broadcasted_iota(jnp.int32, (32, width), 1) // rows
+        owner = lax.broadcasted_iota(jnp.int32, (32, width), 0)
+        for j in range(gain.shape[0]):
+            if p == 0:
+                wanted = block * 4 + j
+            elif p == 1:
+                wanted = (block // 4) * 16 + j * 4 + lax.rem(block, 4)
+            else:
+                wanted = j * 16 + block
+            gain[j] = jnp.sum(jnp.where(owner == wanted, spread, 0.0), axis=0, keepdims=True)
+
+    users_here, heads_here = query.shape[0], query.shape[1]
+    loads[0].wait()
+    wide = heads_here * ROPE
+    owner = lax.broadcasted_iota(jnp.int32, (heads_here, wide), 1) // ROPE
+    mask = owner == lax.broadcasted_iota(jnp.int32, (heads_here, wide), 0)
+    fold = lax.rem(lax.broadcasted_iota(jnp.int32, (wide, ROPE), 0), ROPE)
+    fold = (fold == lax.broadcasted_iota(jnp.int32, (wide, ROPE), 1)).astype(F32).astype(BF16)
+    for r in range(users_here):
+        row = jnp.broadcast_to(rope[r : r + 1, :].astype(F32), (heads_here, wide))
+        row = jnp.where(mask, row, 0.0).astype(BF16)
+        positional[r] = jnp.dot(row, fold, preferred_element_type=F32).astype(BF16)
+    loads[1].wait()
+    history = cache.shape[1]
+    moment = lax.broadcasted_iota(jnp.int32, (heads_here, history), 1)
+
+    def attend(step, carry):
+        slot = lax.rem(step, 2)
+        for copy in user_loads(step):
+            copy.wait()
+        weights = []
+        for n in range(GROUP):
+            r = step * GROUP + n
+            place = slot * GROUP + n
+            scores = lax.dot_general(
+                query[r], cache[place], (((1,), (1,)), ((), ())), preferred_element_type=F32
+            )
+            scores += jnp.dot(positional[r], keys[place], preferred_element_type=F32)
+            scores = scores * (NOPE + ROPE) ** (-0.5)
+            scores = jnp.where(moment < lengths_ref[r], scores, -1e30)
+            exponent = jnp.exp(scores - jnp.max(scores, axis=-1, keepdims=True))
+            weights.append((exponent / jnp.sum(exponent, axis=-1, keepdims=True)).astype(BF16))
+        for n in range(GROUP):
+            r = step * GROUP + n
+            value = jnp.dot(weights[n], cache[slot * GROUP + n], preferred_element_type=F32)
+            value = value.astype(BF16).astype(F32)
+            rows = pl.ds(pl.multiple_of(r * heads_here, heads_here), heads_here)
+            for t in range(context.shape[0]):
+                context[t, rows, :] = value[:, t * LANES : (t + 1) * LANES]
+
+        @pl.when(step < users_here // GROUP - 2)
+        def _():
+            for copy in user_loads(step + 2):
+                copy.start()
+
+        return carry
+
+    lax.fori_loop(0, users_here // GROUP, attend, 0)
+    loads[2].wait()
+
+    def head_value(h):
+        tiles = [context[t, pl.ds(h, users_here, stride=heads_here), :] for t in range(context.shape[0])]
+        rows = jnp.concatenate(tiles, axis=1).astype(BF16)
+        value = jnp.dot(rows, value_up[h], preferred_element_type=F32)
+        return value.astype(BF16)
 
     order = (("y", "z"), ("z", "y"))
-    half = heads0.shape[-1]
 
     def head_block(p, k, **index):
         place = {"x": lax.rem(x_lo + k, 2), "y": me["y"], "z": me["z"]}
@@ -132,9 +215,11 @@
         return at(heads[p], **index)
 
     for p in range(2):
-        loads[p].wait()
+        for h in range(heads_here // 2):
+            heads[p][x_lo, me["y"], me["z"], :, h * 128 : h * 128 + 128] = head_value(p * (heads_here // 2) + h)
+        if p == 0:
+            pl.semaphore_wait(barrier, len(around))
         send(("hx", p), own_heads[p], own_heads[p], x_lo_partner)
-    for p in range(2):
         b, c = order[p]
         for by in (1, 3):
             send(("hb", p, 0, by), own_heads[p], own_heads[p], neighbour(b, by))
@@ -143,14 +228,12 @@
     gains = (gain0, gain1, gain2)
 
     def transpose_part(p, which):
-        source = (gate_in, up_in)[which]
-
         def step(j, carry):
-            block = weight_plane(source, p, j).T.astype(F32) * gains[p][j]
-            wts[p][0, j, which * 256 : which * 256 + 256, :] = block.astype(BF16)
+            block = weight_plane(weight_in, p, j).T.astype(F32) * gains[p][j]
+            wts[p][j, 0, which * 256 : which * 256 + 256, :] = block.astype(BF16)
             return carry
 
-        lax.fori_loop(0, wts[p].shape[1], step, 0)
+        lax.fori_loop(0, wts[p].shape[0], step, 0)
 
     def transpose_down():
         def step(j, carry):
@@ -161,37 +244,28 @@
         lax.fori_loop(0, 8, step, 0)
 
     def share_part(p):
-        send(("wt", p), wts[p].at[0], wts[p].at[1], partner)
-
-    def task_first():
-        loads[2].wait()
-        loads[3].wait()
-        transpose_part(0, 0)
-
-    def task_1():
-        transpose_part(0, 1)
-        share_part(0)
-
-    def task_2():
-        transpose_part(1, 0)
-
-    def task_3():
-        transpose_part(1, 1)
-        share_part(1)
-
-    def task_4():
-        transpose_part(2, 0)
-
-    def task_5():
-        transpose_part(2, 1)
-        share_part(2)
-
-    def task_6():
+        send(("wt", p), wts[p].at[:, 0], wts[p].at[:, 1], partner)
+
+    def gate_task(p):
+        if p == 0:
+            loads[3].wait()
+        transpose_part(p, 0)
+        if p == 2:
+            loads[7].start()
+
+    def up_task(p):
+        if p == 0:
+            loads[7].wait()
+        transpose_part(p, 1)
+        share_part(p)
+
+    def down_task():
         loads[5].wait()
         transpose_down()
         send(("dn",), downt.at[0], downt.at[1], partner)
 
-    tasks = [task_first, task_1, task_2, task_3, task_4, task_5, task_6]
+    tasks = [functools.partial(gate_task, p) for p in range(3)] + [down_task]
+    tasks += [functools.partial(up_task, p) for p in range(3)]
 
     def work():
         if tasks:
@@ -240,7 +314,9 @@
         c = order[p][1]
         j = shift(c, by)
         rows = get(heads[p], **{c: j}).reshape(-1, half)
-        product = jnp.dot(rows, out_proj[p * half : (p + 1) * half, :], preferred_element_type=F32)
+        product = lax.dot_general(
+            rows, out_proj[:, p * half : (p + 1) * half], (((1,), (1,)), ((), ())), preferred_element_type=F32
+        )
         product = product.reshape(2, 4, 16, FEATS)
         if c == "z":
             attn[:, :, j] = product
@@ -276,10 +352,11 @@
     far_out[...] = (attn_mine[1 - x_hi] + pair_in[1 - x_hi]).astype(BF16)
     send(("far",), far_out, far_in, neighbour("x", 2))
     loads[6].wait()
-    near = (attn_mine[x_hi] + pair_in[x_hi]).reshape(LANES, FEATS) + hidden[...].astype(F32)
+    near = (attn_mine[x_hi] + pair_in[x_hi]).reshape(LANES, FEATS)
     recv(("far",), far_in)
     residual = near + far_in[...].reshape(LANES, FEATS).astype(F32)
     residual = jnp.concatenate([residual, jnp.zeros((LANES, 32), F32)], axis=1).T[:FEATS]
+    residual = residual + hidden[...].astype(F32)
     out_ref[...] = residual
     routed = residual.astype(BF16)
 
@@ -326,14 +403,24 @@
     for p in range(3):
         plane_group(p, 3)
         plane_group(p, 1)
+    def pass_on(m):
+        for p in range(3):
+            a, b, c = axes[p]
+            for by in (1, 3):
+                region = at(rts[p], **{b: shift(b, m), c: shift(c, -by)})
+                recv(("gc", p, m, by), region)
+                if (m in (0, 1)) == (by == 1):
+                    send(("gd", p, m), region, region, neighbour(c, by))
+
     for p in range(3):
         a, b, c = axes[p]
         for k in (0, 1, 3, 2):
             recv(("gf", p, k), spot(p, **{a: shift(a, k), b: shift(b, 2)}))
         plane_group(p, 2)
-
-    for p in range(3):
-        recv(("wt", p), wts[p].at[1])
+    pass_on(0)
+
+    for p in range(3):
+        recv(("wt", p), wts[p].at[:, 1])
     totals = {"square": jnp.zeros((1, 256), F32), "first": True}
 
     def users_of(p, by):
@@ -357,24 +444,18 @@
         rows = users_of(p, by)
         wide = rows.astype(F32)
         totals["square"] = totals["square"] + jnp.sum(wide * wide, axis=0, keepdims=True)
-        for slot in range(2):
-            product = jnp.dot(wts[p][slot, plane_of(p, by)], rows, preferred_element_type=F32)
-            if totals["first"]:
-                gate_up[slot] = product
-            else:
-                gate_up[slot] += product
+        weight = wts[p][plane_of(p, by)]
+        product = jnp.dot(weight.reshape(1024, weight.shape[-1]), rows, preferred_element_type=F32)
+        if totals["first"]:
+            gate_up[...] = product
+        else:
+            gate_up[...] += product
         totals["first"] = False
 
     multiply(0, 0)
     multiply(1, 0)
-    for m in (0, 1, 3, 2):
-        for p in range(3):
-            a, b, c = axes[p]
-            for by in (1, 3):
-                region = at(rts[p], **{b: shift(b, m), c: shift(c, -by)})
-                recv(("gc", p, m, by), region)
-                if (m in (0, 1)) == (by == 1):
-                    send(("gd", p, m), region, region, neighbour(c, by))
+    for m in (1, 3, 2):
+        pass_on(m)
     for by in (1, 3):
         multiply(0, by)
         multiply(1, by)
@@ -387,8 +468,8 @@
 
     scale = lax.rsqrt(totals["square"] * (1.0 / (32 * FEATS)) + norm_eps)
     for slot in range(2):
-        gate = gate_up[slot, 0:256] * scale
-        upward = gate_up[slot, 256:512] * scale
+        gate = gate_up[slot * 512 : slot * 512 + 256] * scale
+        upward = gate_up[slot * 512 + 256 : slot * 512 + 512] * scale
         act[slot * 256 : slot * 256 + 256] = (gate / (1.0 + jnp.exp(-gate)) * upward).astype(BF16)
 
     recv(("dn",), downt.at[1])
@@ -396,7 +477,12 @@
     r1, r2, r3, r4, r5 = (
         (r1_0, r1_1, r1_2), (r2_0, r2_1, r2_2), (r3_0, r3_1, r3_2), (r4_0, r4_1, r4_2), (r5_0, r5_1, r5_2)
     )
-    share = jnp.concatenate([share_ref[core], share_ref[core + 2]], axis=1)
+    share = jnp.sum(jnp.where(ids_ref[...] == dev, weights_ref[...], 0.0), axis=0, keepdims=True)
+    share = jnp.where(
+        core == 0,
+        jnp.concatenate([share[:, 0:128], share[:, 256:384]], axis=1),
+        jnp.concatenate([share[:, 128:256], share[:, 384:512]], axis=1),
+    )
 
     def down(p, by):
         first, rows, _ = PARTS[p]
@@ -496,82 +582,62 @@
         out_ref[first : first + rows, :] = total
     for copy in sent:
         copy.wait_send()
-    print("messages", len(tags))
-
-
-def remote_part(head_values, output_proj, hidden, gains, share, gate, up, down):
+
+
+def body(
+    query_latent, query_rope, cache_latent, cache_rope, lengths, value_up, output_proj, hidden,
+    norm_gain, route_ids, route_weights, gate_proj, up_proj, down_proj,
+):
     def bf(*shape):
         return pltpu.VMEM(shape, BF16)
 
     def f32(*shape):
         return pltpu.VMEM(shape, F32)
 
+    users, heads, latent = query_latent.shape
+    history = cache_latent.shape[1]
+    half = heads * LANES // 2
     rows = [r for _, r, _ in PARTS]
-    any_space = pl.BlockSpec(memory_space=pl.ANY)
+    hbm = pl.BlockSpec(memory_space=pl.ANY)
     vmem = pl.BlockSpec(memory_space=pltpu.VMEM)
-    half = head_values.shape[-1]
     scratch = [
-        bf(2, 4, 4, 16, half), bf(2, 4, 4, 16, half), bf(*output_proj.shape), f32(2, 4, 4, 16, FEATS),
-        f32(2, 2, 4, 16, FEATS), bf(2, 4, 16, FEATS), bf(2, 4, 16, FEATS), bf(LANES, FEATS),
-        bf(2, 4, 4, FEATS, 256), bf(2, 4, 4, FEATS, 256), bf(256, 32 * FEATS),
-        bf(2, 4, 512, 640), bf(2, 4, 512, 640), bf(2, 2, 512, 1024), bf(2, 2, 4, 4, FEATS, 256),
+        bf(users, heads, latent), bf(users, heads * ROPE), bf(users, heads, ROPE),
+        bf(2 * GROUP, history, latent), bf(2 * GROUP, ROPE, history), f32(latent // LANES, users * heads, LANES),
+        bf(*value_up.shape),
+        bf(2, 4, 4, 16, half), bf(2, 4, 4, 16, half), bf(FEATS, 2 * half), f32(2, 4, 4, 16, FEATS),
+        f32(2, 2, 4, 16, FEATS), bf(2, 4, 16, FEATS), bf(2, 4, 16, FEATS), bf(FEATS, LANES),
+        bf(2, 4, 4, FEATS, 256), bf(256, 32 * FEATS),
+        f32(4, 1, 640), f32(4, 1, 640), f32(2, 1, 1024),
+        bf(4, 2, 512, 640), bf(4, 2, 512, 640), bf(2, 2, 512, 1024), bf(2, 2, 4, 4, FEATS, 256),
         *[bf(4, 4, 4, r, LANES) for r in rows],
-        f32(2, 512, 256), bf(512, 256),
+        f32(1024, 256), bf(512, 256),
         *[bf(4, 4, 4, r, LANES) for r in rows],
         *[bf(4, 4, r, LANES) for r in rows],
         *[bf(2, 4, 4, r, LANES) for r in rows],
         *[bf(4, r, LANES) for r in rows],
         *[bf(2, 4, r, LANES) for r in rows],
         *[bf(3, r, LANES) for r in rows],
-        pltpu.SemaphoreType.DMA((7,)),
+        pltpu.SemaphoreType.DMA((2, 2)),
+        pltpu.SemaphoreType.DMA((8,)),
         pltpu.SemaphoreType.DMA((256,)),
         pltpu.SemaphoreType.DMA((256,)),
     ]
-    return pl.pallas_call(
-        moe_kernel,
+    out = pl.pallas_call(
+        layer_kernel,
         out_shape=jax.ShapeDtypeStruct((FEATS, LANES), F32),
-        in_specs=[any_space, any_space, any_space, vmem, vmem, vmem, vmem, any_space, any_space, any_space],
+        in_specs=[
+            hbm, hbm, hbm, hbm, pl.BlockSpec(memory_space=pltpu.SMEM), hbm,
+            hbm, hbm, vmem, vmem, vmem, hbm, hbm, hbm,
+        ],
         out_specs=vmem,
         scratch_shapes=scratch,
         compiler_params=pltpu.CompilerParams(
-            collective_id=0, has_side_effects=True, vmem_limit_bytes=60 * 1024 * 1024
+            collective_id=0, has_side_effects=True, vmem_limit_bytes=63 * 1024 * 1024
         ),
-        cost_estimate=pl.CostEstimate(flops=7 * 10**9, bytes_accessed=16 * 2**20, transcendentals=0),
-    )(head_values, output_proj, hidden, *gains, share, gate, up, down)
-
-
-def body(
-    query_latent, query_rope, cache_latent, cache_rope, lengths, value_up, output_proj, hidden,
-    norm_gain, route_ids, route_weights, gate_proj, up_proj, down_proj,
-):
-    users_here, heads_here, latent_width = query_latent.shape
-    history = cache_latent.shape[1]
-    rope_width = cache_rope.shape[1]
-    positional = query_rope.reshape(users_here, heads_here, rope_width)
-    scores = jnp.einsum(
-        "rhc,rtc->rht", query_latent, cache_latent, preferred_element_type=jnp.float32
-    )
-    scores = scores + jnp.einsum(
-        "rhe,ret->rht", positional, cache_rope, preferred_element_type=jnp.float32
-    )
-    scores = scores * (NOPE + ROPE) ** (-0.5)
-    visible = jnp.arange(history, dtype=jnp.int32)[None, None, :] < lengths[:, None, None]
-    scores = jnp.where(visible, scores, -1e30)
-    highest = jnp.max(scores, axis=-1, keepdims=True)
-    exponent = jnp.exp(scores - highest)
-    attn_weights = (exponent / jnp.sum(exponent, axis=-1, keepdims=True)).astype(jnp.bfloat16)
-    context = jnp.einsum(
-        "rht,rtc->rhc", attn_weights, cache_latent, preferred_element_type=jnp.float32
-    ).astype(jnp.bfloat16)
-    head_values = jnp.einsum(
-        "rhc,hcv->rhv", context, value_up, preferred_element_type=jnp.float32
-    ).astype(jnp.bfloat16)
-    head_values = head_values.reshape(users_here, 2, -1).transpose(1, 0, 2)
-
-    expert = lax.axis_index("dev")
-    share = jnp.sum(jnp.where(route_ids == expert, route_weights, 0.0), axis=1).reshape(4, 1, LANES)
-    out = remote_part(
-        head_values, output_proj, hidden, gain_planes(norm_gain), share,
+        cost_estimate=pl.CostEstimate(flops=9 * 10**9, bytes_accessed=27 * 2**20, transcendentals=0),
+    )(
+        query_latent, query_rope, cache_latent, cache_rope, lengths, value_up,
+        output_proj.T, hidden.T, norm_gain.reshape(32, FEATS), route_ids.T, route_weights.T,
         gate_proj.reshape(2, 4, 4, FEATS, 256), up_proj.reshape(2, 4, 4, FEATS, 256), down_proj[0],
     )
     return out.T.astype(BF16)

time: 119 us -> 109 us (0.916)
  Pallas kernels: 90.9 us -> 106 us
  matrix products: 14.6 us -> 0 us
  local copies, waits for them, and re-layouts: 9.17 us -> 1.44 us
  other arithmetic: 3.97 us -> 1.53 us
    pallas_call x1, Pallas kernels: 90.9 us -> 106 us  [body(): pl.pallas_call(layer_kernel, out_shape=jax.ShapeDtypeStruct((FEATS, LANES...]
    dot_general x4 -> x0, matrix products: 14.6 us -> none  [the longest x1 6.09 us: body(): jnp.einsum('rhc,rtc->rht', query_latent, cache_latent, preferred_element_...]
    unnamed x6 -> x0, local copies, waits for them, and re-layouts: 4.31 us -> none
    reshape x7 -> x1, local copies, waits for them, and re-layouts: 4.66 us -> 1.44 us  [body(): norm_gain.reshape(32, FEATS)]
    reduce_sum x1 -> x0, other arithmetic: 1.41 us -> none  [body(): jnp.sum(jnp.where(route_ids == expert, route_weights, 0.0), axis=1)]
where the time goes in v2:
time: 109 us
  Pallas kernels  106 us (97%)
  other arithmetic  1.53 us (1%)
  local copies, waits for them, and re-layouts  1.44 us (1%)
    pallas_call x1, Pallas kernels, body(): pl.pallas_call(layer_kernel, out_shape=jax.ShapeDtypeStruct((FEATS, LANES...  106 us

profile of v2, /device:TPU:0, one launch (start us, length us, event | category | flops | bytes accessed | tf_op | source)
XLA Modules:
  0.0 108.8 jit_solution(1980868655143333092)
XLA Ops:
  0.0 1.4 %reshape.9.gain_ref = f32[32,224]{1,0:T(8,128)} reshape(f32[7168]{0:T(1024)} %param.22) | data formatting | bytes 57344 | tf_op jit(solution)/shard_map/reshape | solution.py:640
  1.4 105.9 %shard_map.136 = f32[224,128]{1,0:T(8,128)} custom-call(bf16[16,32,512]{2,1,0:T(8,128)(2,1)} %query_hbm.1, bf16[16,2048]{1,0:T(8,128)(2,1)} %rope_hbm.1, bf16[16,512,512]{2,1,0:T(8,128)(2,1)} %cache_hbm.1, bf16[16,64,512]{2,1,0:T(8,128)(2,1)} %keys_hbm.1, s32[16]{0:T(128)} %lengths_ref.1, bf16[32,512,128]{2,1,0:T(8,128)(2,1)} %value_up_hbm.1, ...), custom_call_target="tpu_custom_call" | custom-call | flops 8999999488 | bytes 28311552 | tf_op jit(solution)/shard_map/pallas_call | solution.py:625
  107.3 1.5 %convert_bitcast_fusion = bf16[128,224]{0,1:T(8,128)(2,1)} fusion(f32[224,128]{1,0:T(8,128)} %shard_map.136), kind=kLoop, calls=%fused_computation | loop fusion | flops 28672 | bytes 172032 | tf_op jit(solution)/shard_map/convert_element_type | solution.py:643

commit v3 on v2

--- a/solution.py
+++ b/solution.py
@@ -42,13 +42,13 @@
 def layer_kernel(
     query_hbm, rope_hbm, cache_hbm, keys_hbm, lengths_ref, value_up_hbm,
     out_proj_hbm, hidden_hbm, gain_ref, ids_ref, weights_ref, gate_hbm, up_hbm, down_hbm,
-    out_ref,
+    out_ref, gate_far, up_far, down_far,
     query, rope, positional, cache, keys, context, value_up,
     heads0, heads1, out_proj, attn, pair_in, far_in, far_out, hidden,
     weight_in, down_in, gain0, gain1, gain2, wt0, wt1, wt2, downt,
     rt0, rt1, rt2, gate_up, act, o0, o1, o2,
     r1_0, r1_1, r1_2, r2_0, r2_1, r2_2, r3_0, r3_1, r3_2, r4_0, r4_1, r4_2, r5_0, r5_1, r5_2,
-    cache_sem, local_sem, send_sem, recv_sem,
+    kept, cache_sem, local_sem, stage_sem, send_sem, recv_sem,
 ):
     sec = lax.axis_index("sec")
     dev = lax.axis_index("dev")
@@ -83,18 +83,23 @@
     def send(tag, src, dst, to):
         i = number(tag)
         copy = pltpu.make_async_remote_copy(
-            src_ref=src, dst_ref=dst, send_sem=send_sem.at[i], recv_sem=recv_sem.at[i],
+            src_ref=src, dst_ref=dst, send_sem=send_sem.at[len(sent)], recv_sem=recv_sem.at[i],
             device_id=to, device_id_type=MESH,
         )
         copy.start()
         sent.append(copy)
 
+    def drain():
+        while sent:
+            sent.pop().wait_send()
+
     def recv(tag, region):
         i = number(tag)
         pltpu.make_async_remote_copy(
-            src_ref=region, dst_ref=region, send_sem=send_sem.at[i], recv_sem=recv_sem.at[i],
+            src_ref=region, dst_ref=region, send_sem=send_sem.at[0], recv_sem=recv_sem.at[i],
             device_id=partner, device_id_type=MESH,
         ).wait_recv()
+
 
     around = [neighbour(axis, by) for axis in "xyz" for by in (1, 2, 3)] + [partner]
     barrier = pltpu.get_barrier_semaphore()
@@ -113,6 +118,19 @@
             pltpu.make_async_copy(cache_hbm.at[users], cache.at[place], cache_sem.at[slot, 0]),
             pltpu.make_async_copy(keys_hbm.at[users], keys.at[place], cache_sem.at[slot, 1]),
         )
+
+    def stage_up(source, n):
+        copies = []
+        for p, (first, rows, _) in enumerate(PARTS):
+            for q in range(2):
+                copies.append(
+                    pltpu.make_async_copy(
+                        source.at[:, :, :, pl.ds(first, rows), pl.ds(q * LANES, LANES)],
+                        (o0, o1, o2)[p].at[pl.ds(2 * q, 2)],
+                        stage_sem.at[n, 2 * p + q],
+                    )
+                )
+        return copies
 
     loads = [
         pltpu.make_async_copy(rope_hbm, rope, local_sem.at[0]),
@@ -122,32 +140,34 @@
         pltpu.make_async_copy(out_proj_hbm, out_proj, local_sem.at[4]),
         pltpu.make_async_copy(down_hbm, down_in, local_sem.at[5]),
         pltpu.make_async_copy(my_hidden, hidden, local_sem.at[6]),
-        pltpu.make_async_copy(up_hbm, weight_in, local_sem.at[7]),
+        pltpu.make_async_copy(gate_far, weight_in, local_sem.at[7]),
+        pltpu.make_async_copy(down_far, down_in, local_sem.at[8]),
     ]
+    up_loads = stage_up(up_hbm, 0), stage_up(up_far, 1)
     for copy in (loads[0], loads[1], *user_loads(0), *user_loads(1)):
         copy.start()
-    for n in (2, 3, 4, 5, 6):
-        loads[n].start()
+    loads[2].start()
 
     for p, gain in enumerate((gain0, gain1, gain2)):
         first, rows, _ = PARTS[p]
         width = gain.shape[-1]
-        column = lax.broadcasted_iota(jnp.int32, (rows, width), 1)
-        spread = (lax.rem(column, rows) == lax.broadcasted_iota(jnp.int32, (rows, width), 0)).astype(F32)
-        spread = jnp.dot(
-            gain_ref[:, first : first + rows], spread,
-            preferred_element_type=F32, precision=lax.Precision.HIGHEST,
-        )
-        block = lax.broadcasted_iota(jnp.int32, (32, width), 1) // rows
-        owner = lax.broadcasted_iota(jnp.int32, (32, width), 0)
+        block = lax.broadcasted_iota(jnp.int32, (LANES, width), 1) // rows
+        offset = lax.rem(lax.broadcasted_iota(jnp.int32, (LANES, width), 1), rows) + first
+        lane = lax.broadcasted_iota(jnp.int32, (LANES, width), 0)
         for j in range(gain.shape[0]):
             if p == 0:
-                wanted = block * 4 + j
+                owner = block * 4 + j
             elif p == 1:
-                wanted = (block // 4) * 16 + j * 4 + lax.rem(block, 4)
+                owner = (block // 4) * 16 + j * 4 + lax.rem(block, 4)
             else:
-                wanted = j * 16 + block
-            gain[j] = jnp.sum(jnp.where(owner == wanted, spread, 0.0), axis=0, keepdims=True)
+                owner = j * 16 + block
+            place = owner * FEATS + offset
+            spread = jnp.dot(
+                gain_ref[...], (lax.rem(place, LANES) == lane).astype(F32),
+                preferred_element_type=F32, precision=lax.Precision.HIGHEST,
+            )
+            held = (place // LANES)[:56] == lane[:56]
+            gain[j] = jnp.sum(jnp.where(held, spread, 0.0), axis=0, keepdims=True)
 
     users_here, heads_here = query.shape[0], query.shape[1]
     loads[0].wait()
@@ -195,7 +215,14 @@
 
         return carry
 
-    lax.fori_loop(0, users_here // GROUP, attend, 0)
+    lax.fori_loop(0, 1, attend, 0)
+    pl.semaphore_wait(barrier, len(around))
+    send(("wg",), gate_hbm, gate_far, partner)
+    send(("wu",), up_hbm, up_far, partner)
+    send(("wd",), down_hbm, down_far, partner)
+    lax.fori_loop(1, users_here // GROUP, attend, 0)
+    for copy in (loads[3], *up_loads[0], *loads[4:7]):
+        copy.start()
     loads[2].wait()
 
     def head_value(h):
@@ -217,8 +244,6 @@
     for p in range(2):
         for h in range(heads_here // 2):
             heads[p][x_lo, me["y"], me["z"], :, h * 128 : h * 128 + 128] = head_value(p * (heads_here // 2) + h)
-        if p == 0:
-            pl.semaphore_wait(barrier, len(around))
         send(("hx", p), own_heads[p], own_heads[p], x_lo_partner)
         b, c = order[p]
         for by in (1, 3):
@@ -227,51 +252,69 @@
     wts = (wt0, wt1, wt2)
     gains = (gain0, gain1, gain2)
 
-    def transpose_part(p, which):
+    def gate_task(slot, p):
+        if p == 0:
+            loads[7 if slot else 3].wait()
+
         def step(j, carry):
             block = weight_plane(weight_in, p, j).T.astype(F32) * gains[p][j]
-            wts[p][j, 0, which * 256 : which * 256 + 256, :] = block.astype(BF16)
+            wts[p][j, slot, 0:256, :] = block.astype(BF16)
             return carry
 
         lax.fori_loop(0, wts[p].shape[0], step, 0)
-
-    def transpose_down():
+        if slot == 0 and p == 2:
+            recv(("wg",), gate_far)
+            loads[7].start()
+
+    def up_task(slot, p):
+        if p == 0:
+            for copy in up_loads[slot]:
+                copy.wait()
+
+        def step(j, carry):
+            for q in range(2):
+                if p == 0:
+                    block = o0[2 * q : 2 * q + 2, :, j]
+                elif p == 1:
+                    block = o1[2 * q : 2 * q + 2, j]
+                else:
+                    block = o2[2 * q + j]
+                block = block.reshape(-1, LANES).T.astype(F32) * gains[p][j]
+                wts[p][j, slot, 256 + q * LANES : 256 + (q + 1) * LANES, :] = block.astype(BF16)
+            return carry
+
+        lax.fori_loop(0, wts[p].shape[0], step, 0)
+        if slot == 1 and p == 0:
+            recv(("wd",), down_far)
+            loads[8].start()
+        if slot == 0 and p == 2:
+            recv(("wu",), up_far)
+            for copy in up_loads[1]:
+                copy.start()
+
+    def down_task(slot, half_of):
+        if half_of == 0:
+            loads[8 if slot else 5].wait()
+
         def step(j, carry):
             block = down_in[:, pl.ds(pl.multiple_of(j * 896, 896), 896)].T
-            downt[0, j // 4, lax.rem(j, 4)] = block.reshape(4, FEATS, 256)
+            downt[slot, j // 4, lax.rem(j, 4)] = block.reshape(4, FEATS, 256)
             return carry
 
-        lax.fori_loop(0, 8, step, 0)
-
-    def share_part(p):
-        send(("wt", p), wts[p].at[:, 0], wts[p].at[:, 1], partner)
-
-    def gate_task(p):
-        if p == 0:
-            loads[3].wait()
-        transpose_part(p, 0)
-        if p == 2:
-            loads[7].start()
-
-    def up_task(p):
-        if p == 0:
-            loads[7].wait()
-        transpose_part(p, 1)
-        share_part(p)
-
-    def down_task():
-        loads[5].wait()
-        transpose_down()
-        send(("dn",), downt.at[0], downt.at[1], partner)
-
-    tasks = [functools.partial(gate_task, p) for p in range(3)] + [down_task]
-    tasks += [functools.partial(up_task, p) for p in range(3)]
-
-    def work():
-        if tasks:
-            tasks.pop(0)()
-
-    work()
+        lax.fori_loop(4 * half_of, 4 * half_of + 4, step, 0)
+
+    tasks = []
+    for slot in range(2):
+        tasks += [functools.partial(gate_task, slot, p) for p in range(3)]
+        tasks += [functools.partial(up_task, slot, p) for p in range(3)]
+        tasks += [functools.partial(down_task, slot, n) for n in range(2)]
+
+    def work(count=1):
+        for task in tasks[:count]:
+            task()
+        del tasks[:count]
+
+    work(8)
 
     def slab_sends(p, m):
         b, c = order[p]
@@ -292,21 +335,20 @@
         b, c = order[p]
         block = head_block(p, 0, **{b: shift(b, 3)})
         recv(("hb", p, 0, 1), block)
-        send(("hf", p, 0), block, block, neighbour(b, 1))
+        send(("hf", p), block, block, neighbour(b, 1))
         recv(("hb", p, 0, 3), head_block(p, 0, **{b: shift(b, 1)}))
     for p in range(2):
         b, c = order[p]
         block = head_block(p, 1, **{b: shift(b, 1)})
         recv(("hb", p, 1, 3), block)
-        send(("hf", p, 1), block, block, neighbour(b, 3))
+        send(("hf", p), block, block, neighbour(b, 3))
         slab_sends(p, 1)
         recv(("hb", p, 1, 1), head_block(p, 1, **{b: shift(b, 3)}))
         slab_sends(p, 3)
     work()
     for p in range(2):
         b, c = order[p]
-        for k in range(2):
-            recv(("hf", p, k), head_block(p, k, **{b: shift(b, 2)}))
+        recv(("hf", p), head_slab(p, **{b: shift(b, 2), c: me[c]}))
         slab_sends(p, 2)
     work()
 
@@ -332,19 +374,17 @@
                 region = head_slab(p, **{b: shift(b, m), c: shift(c, -by)})
                 recv(("hc", p, m, by), region)
                 if (m in (0, 1)) == (by == 1):
-                    send(("hd", p, m), region, region, neighbour(c, by))
+                    send(("hd", p), region, region, neighbour(c, by))
         work()
-    while tasks:
-        work()
+    work(len(tasks))
     project(0, 1)
     project(0, 3)
-    for m in (0, 3, 1, 2):
-        for p in range(2):
-            b, c = order[p]
-            recv(("hd", p, m), head_slab(p, **{b: shift(b, m), c: shift(c, 2)}))
+    recv(("hd", 0), head_slab(0, **{order[0][1]: shift(order[0][1], 2)}))
     project(0, 2)
-    for by in (0, 1, 3, 2):
+    for by in (0, 1, 3):
         project(1, by)
+    recv(("hd", 1), head_slab(1, **{order[1][1]: shift(order[1][1], 2)}))
+    project(1, 2)
 
     attn_mine = attn.at[:, pl.ds(core * 2, 2)]
     send(("pair",), attn.at[:, pl.ds((1 - core) * 2, 2)], pair_in, partner)
@@ -357,7 +397,7 @@
     residual = near + far_in[...].reshape(LANES, FEATS).astype(F32)
     residual = jnp.concatenate([residual, jnp.zeros((LANES, 32), F32)], axis=1).T[:FEATS]
     residual = residual + hidden[...].astype(F32)
-    out_ref[...] = residual
+    kept[...] = residual
     routed = residual.astype(BF16)
 
     rts = (rt0, rt1, rt2)
@@ -370,6 +410,7 @@
         return at(rts[p], **place)
 
     axes = [tuple(o) for _, _, o in PARTS]
+    drain()
     for p in range(3):
         a, b, c = axes[p]
         for by in (1, 3, 2):
@@ -399,7 +440,7 @@
                 block = spot(p, **{a: shift(a, k), b: shift(b, -by)})
                 recv(("gb", p, k, by), block)
                 if (k in (0, 1)) == (by == 1):
-                    send(("gf", p, k), block, block, neighbour(b, by))
+                    send(("gf", p), block, block, neighbour(b, by))
     for p in range(3):
         plane_group(p, 3)
         plane_group(p, 1)
@@ -410,17 +451,14 @@
                 region = at(rts[p], **{b: shift(b, m), c: shift(c, -by)})
                 recv(("gc", p, m, by), region)
                 if (m in (0, 1)) == (by == 1):
-                    send(("gd", p, m), region, region, neighbour(c, by))
+                    send(("gd", p), region, region, neighbour(c, by))
 
     for p in range(3):
         a, b, c = axes[p]
-        for k in (0, 1, 3, 2):
-            recv(("gf", p, k), spot(p, **{a: shift(a, k), b: shift(b, 2)}))
+        recv(("gf", p), spot(p, **{a: slice(None), b: shift(b, 2)}))
         plane_group(p, 2)
     pass_on(0)
 
-    for p in range(3):
-        recv(("wt", p), wts[p].at[:, 1])
     totals = {"square": jnp.zeros((1, 256), F32), "first": True}
 
     def users_of(p, by):
@@ -462,8 +500,7 @@
     multiply(2, 1)
     for p in range(3):
         a, b, c = axes[p]
-        for m in (0, 3, 1, 2):
-            recv(("gd", p, m), at(rts[p], **{b: shift(b, m), c: shift(c, 2)}))
+        recv(("gd", p), at(rts[p], **{c: shift(c, 2)}))
         multiply(p, 2 if p < 2 else 0)
 
     scale = lax.rsqrt(totals["square"] * (1.0 / (32 * FEATS)) + norm_eps)
@@ -472,7 +509,7 @@
         upward = gate_up[slot * 512 + 256 : slot * 512 + 512] * scale
         act[slot * 256 : slot * 256 + 256] = (gate / (1.0 + jnp.exp(-gate)) * upward).astype(BF16)
 
-    recv(("dn",), downt.at[1])
+    drain()
     outs = (o0, o1, o2)
     r1, r2, r3, r4, r5 = (
         (r1_0, r1_1, r1_2), (r2_0, r2_1, r2_2), (r3_0, r3_1, r3_2), (r4_0, r4_1, r4_2), (r5_0, r5_1, r5_2)
@@ -517,9 +554,9 @@
         else:
             down(p, 1)
         for m in (2, 3):
-            send(("s2", p, 0, m), o_slab(p, 1, m), r2[p].at[0, m], neighbour(c, 1))
+            send(("s2", p, m), o_slab(p, 1, m), r2[p].at[m, 0], neighbour(c, 1))
         for m in (1, 0):
-            send(("s2", p, 1, m), o_slab(p, 3, m), r2[p].at[1, m], neighbour(c, 3))
+            send(("s2", p, m), o_slab(p, 3, m), r2[p].at[m, 1], neighbour(c, 3))
     for p in range(2):
         down(p, 0)
 
@@ -534,54 +571,50 @@
             side = 0 if by == 1 else 1
             slab = o_slab(p, by, m)
             add_to(slab, r1[p].at[m])
-            send(("s2", p, side, m), slab, r2[p].at[side, m], neighbour(c, by))
+            send(("s2", p, m), slab, r2[p].at[m, side], neighbour(c, by))
 
     for m in (2, 1, 3, 0):
         for p in range(3):
             a, b, c = axes[p]
             slab = o_slab(p, 0, m)
-            for side in range(2):
-                recv(("s2", p, side, m), r2[p].at[side, m])
+            recv(("s2", p, m), r2[p].at[m])
             slab[...] = (
-                slab[...].astype(F32) + r2[p][0, m].astype(F32) + r2[p][1, m].astype(F32)
+                slab[...].astype(F32) + r2[p][m, 0].astype(F32) + r2[p][m, 1].astype(F32)
             ).astype(BF16)
             if m == 2:
                 send(("s3", p, 0), slab.at[0:2], r3[p].at[0:2], neighbour(b, 1))
                 send(("s3", p, 1), slab.at[2:4], r3[p].at[2:4], neighbour(b, 3))
             elif m == 1:
-                send(("s4", p, 0, 1), slab.at[2:4], r4[p].at[0, 2:4], neighbour(b, 1))
+                send(("s4", p), slab.at[2:4], r4[p].at[0, 2:4], neighbour(b, 1))
             elif m == 3:
-                send(("s4", p, 1, 0), slab.at[0:2], r4[p].at[1, 0:2], neighbour(b, 3))
+                send(("s4", p), slab.at[0:2], r4[p].at[1, 0:2], neighbour(b, 3))
     for p in range(3):
         a, b, c = axes[p]
         recv(("s3", p, 0), r3[p].at[0:2])
         slab = o_slab(p, 0, 1).at[0:2]
         add_to(slab, r3[p].at[0:2])
-        send(("s4", p, 0, 0), slab, r4[p].at[0, 0:2], neighbour(b, 1))
+        send(("s4", p), slab, r4[p].at[0, 0:2], neighbour(b, 1))
         recv(("s3", p, 1), r3[p].at[2:4])
         slab = o_slab(p, 0, 3).at[2:4]
         add_to(slab, r3[p].at[2:4])
-        send(("s4", p, 1, 1), slab, r4[p].at[1, 2:4], neighbour(b, 3))
+        send(("s4", p), slab, r4[p].at[1, 2:4], neighbour(b, 3))
     for p in range(3):
         a, b, c = axes[p]
-        for side in range(2):
-            for lower in range(2):
-                recv(("s4", p, side, lower), r4[p].at[side, 2 * lower : 2 * lower + 2])
+        recv(("s4", p), r4[p])
         slab = o_slab(p, 0, 0)
         slab[...] = (
             slab[...].astype(F32) + r4[p][0].astype(F32) + r4[p][1].astype(F32)
         ).astype(BF16)
         for k in (2, 1, 3):
-            send(("s5", p, k), slab.at[shift(a, k)], r5[p].at[k - 1], neighbour(a, k))
+            send(("s5", p), slab.at[shift(a, k)], r5[p].at[k - 1], neighbour(a, k))
     for p, (first, rows, _) in enumerate(PARTS):
         a = axes[p][0]
-        total = out_ref[first : first + rows, :] + outs[p][me["x"], me["y"], me["z"]].astype(F32)
+        total = kept[first : first + rows, :] + outs[p][me["x"], me["y"], me["z"]].astype(F32)
+        recv(("s5", p), r5[p])
         for k in (1, 3, 2):
-            recv(("s5", p, k), r5[p].at[k - 1])
             total = total + r5[p][k - 1].astype(F32)
-        out_ref[first : first + rows, :] = total
-    for copy in sent:
-        copy.wait_send()
+        out_ref[first : first + rows, :] = total.astype(BF16)
+    drain()
 
 
 def body(
@@ -613,23 +646,31 @@
         f32(1024, 256), bf(512, 256),
         *[bf(4, 4, 4, r, LANES) for r in rows],
         *[bf(4, 4, r, LANES) for r in rows],
-        *[bf(2, 4, 4, r, LANES) for r in rows],
+        *[bf(4, 2, 4, r, LANES) for r in rows],
         *[bf(4, r, LANES) for r in rows],
         *[bf(2, 4, r, LANES) for r in rows],
         *[bf(3, r, LANES) for r in rows],
+        f32(FEATS, LANES),
         pltpu.SemaphoreType.DMA((2, 2)),
-        pltpu.SemaphoreType.DMA((8,)),
-        pltpu.SemaphoreType.DMA((256,)),
-        pltpu.SemaphoreType.DMA((256,)),
+        pltpu.SemaphoreType.DMA((9,)),
+        pltpu.SemaphoreType.DMA((2, 6)),
+        pltpu.SemaphoreType.DMA((81,)),
+        pltpu.SemaphoreType.DMA((134,)),
     ]
-    out = pl.pallas_call(
+    gate_proj = gate_proj.reshape(2, 4, 4, FEATS, 256)
+    up_proj = up_proj.reshape(2, 4, 4, FEATS, 256)
+    down_proj = down_proj[0]
+    out, *_ = pl.pallas_call(
         layer_kernel,
-        out_shape=jax.ShapeDtypeStruct((FEATS, LANES), F32),
+        out_shape=(
+            jax.ShapeDtypeStruct((FEATS, LANES), BF16),
+            *[jax.ShapeDtypeStruct(a.shape, BF16) for a in (gate_proj, up_proj, down_proj)],
+        ),
         in_specs=[
             hbm, hbm, hbm, hbm, pl.BlockSpec(memory_space=pltpu.SMEM), hbm,
             hbm, hbm, vmem, vmem, vmem, hbm, hbm, hbm,
         ],
-        out_specs=vmem,
+        out_specs=(vmem, hbm, hbm, hbm),
         scratch_shapes=scratch,
         compiler_params=pltpu.CompilerParams(
             collective_id=0, has_side_effects=True, vmem_limit_bytes=63 * 1024 * 1024
@@ -637,10 +678,10 @@
         cost_estimate=pl.CostEstimate(flops=9 * 10**9, bytes_accessed=27 * 2**20, transcendentals=0),
     )(
         query_latent, query_rope, cache_latent, cache_rope, lengths, value_up,
-        output_proj.T, hidden.T, norm_gain.reshape(32, FEATS), route_ids.T, route_weights.T,
-        gate_proj.reshape(2, 4, 4, FEATS, 256), up_proj.reshape(2, 4, 4, FEATS, 256), down_proj[0],
+        output_proj.T, hidden.T, norm_gain.reshape(56, LANES), route_ids.T, route_weights.T,
+        gate_proj, up_proj, down_proj,
     )
-    return out.T.astype(BF16)
+    return out.T
 
 
 def solution(mesh):

time: 109 us -> 104 us (0.954)
  Pallas kernels: 106 us -> 102 us
  other arithmetic: 1.53 us -> 0 us
    pallas_call x1, Pallas kernels: 106 us -> 102 us  [body(): pl.pallas_call(layer_kernel, out_shape=(jax.ShapeDtypeStruct((FEATS, LANE...]
    convert_element_type x1 -> x0, other arithmetic: 1.53 us -> none  [body(): return out.T.astype(BF16)]
    unnamed x0 -> x1, local copies, waits for them, and re-layouts: none -> 1.45 us
    reshape x1 -> x0, local copies, waits for them, and re-layouts: 1.44 us -> none  [body(): norm_gain.reshape(32, FEATS)]
where the time goes in v3:
time: 104 us
  Pallas kernels  102 us (98%)
  local copies, waits for them, and re-layouts  1.45 us (1%)
    pallas_call x1, Pallas kernels, body(): pl.pallas_call(layer_kernel, out_shape=(jax.ShapeDtypeStruct((FEATS, LANE...  102 us

profile of v3, /device:TPU:0, one launch (start us, length us, event | category | flops | bytes accessed | tf_op | source)
XLA Modules:
  0.0 103.8 jit_solution(6461057592674096797)
XLA Ops:
  0.0 102.4 %shard_map.136 = (bf16[224,128]{1,0:T(8,128)(2,1)}, bf16[2,4,4,224,256]{4,3,2,1,0:T(8,128)(2,1)}, bf16[2,4,4,224,256]{4,3,2,1,0:T(8,128)(2,1)}, bf16[256,7168]{1,0:T(8,128)(2,1)}) custom-call(bf16[16,32,512]{2,1,0:T(8,128)(2,1)} %query_hbm.1, bf16[16,2048]{1,0:T(8,128)(2,1)} %rope_hbm.1, bf16[16,512,512]{2,1,0:T(8,128)(2,1)} %cache_hbm.1, ...), custom_call_target="tpu_custom_call" | custom-call | flops 8999999488 | bytes 28311552 | tf_op jit(solution)/shard_map/pallas_call | solution.py:663
  102.4 1.4 %copy.16 = bf16[128,224]{0,1:T(8,128)(2,1)} copy(bf16[128,224]{0,1:T(8,128)(2,1)} %bitcast.9) | data formatting | bytes 114688

commit v4 on v3

--- a/solution.py
+++ b/solution.py
@@ -248,6 +248,8 @@
         b, c = order[p]
         for by in (1, 3):
             send(("hb", p, 0, by), own_heads[p], own_heads[p], neighbour(b, by))
+        for by in (1, 3):
+            send(("hc", p, 0, by), own_heads[p], own_heads[p], neighbour(c, by))
 
     wts = (wt0, wt1, wt2)
     gains = (gain0, gain1, gain2)
@@ -262,9 +264,6 @@
             return carry
 
         lax.fori_loop(0, wts[p].shape[0], step, 0)
-        if slot == 0 and p == 2:
-            recv(("wg",), gate_far)
-            loads[7].start()
 
     def up_task(slot, p):
         if p == 0:
@@ -284,13 +283,6 @@
             return carry
 
         lax.fori_loop(0, wts[p].shape[0], step, 0)
-        if slot == 1 and p == 0:
-            recv(("wd",), down_far)
-            loads[8].start()
-        if slot == 0 and p == 2:
-            recv(("wu",), up_far)
-            for copy in up_loads[1]:
-                copy.start()
 
     def down_task(slot, half_of):
         if half_of == 0:
@@ -308,6 +300,15 @@
         tasks += [functools.partial(gate_task, slot, p) for p in range(3)]
         tasks += [functools.partial(up_task, slot, p) for p in range(3)]
         tasks += [functools.partial(down_task, slot, n) for n in range(2)]
+
+    def fetch_partner():
+        recv(("wg",), gate_far)
+        loads[7].start()
+        recv(("wu",), up_far)
+        for copy in up_loads[1]:
+            copy.start()
+        recv(("wd",), down_far)
+        loads[8].start()
 
     def work(count=1):
         for task in tasks[:count]:
@@ -329,8 +330,9 @@
         for by in (1, 3):
             send(("hb", p, 1, by), other, other, neighbour(b, by))
     for p in range(2):
-        slab_sends(p, 0)
-    work()
+        other = head_block(p, 1)
+        for by in (1, 3):
+            send(("hc", p, 0, by), other, other, neighbour(order[p][1], by))
     for p in range(2):
         b, c = order[p]
         block = head_block(p, 0, **{b: shift(b, 3)})
@@ -345,12 +347,11 @@
         slab_sends(p, 1)
         recv(("hb", p, 1, 1), head_block(p, 1, **{b: shift(b, 3)}))
         slab_sends(p, 3)
-    work()
     for p in range(2):
         b, c = order[p]
         recv(("hf", p), head_slab(p, **{b: shift(b, 2), c: me[c]}))
         slab_sends(p, 2)
-    work()
+    fetch_partner()
 
     def project(p, by, first=False):
         c = order[p][1]
@@ -375,7 +376,7 @@
                 recv(("hc", p, m, by), region)
                 if (m in (0, 1)) == (by == 1):
                     send(("hd", p), region, region, neighbour(c, by))
-        work()
+        work(2)
     work(len(tasks))
     project(0, 1)
     project(0, 3)
@@ -417,6 +418,8 @@
             send(("ga", p, by), spot(p), spot(p), neighbour(a, by))
         for by in (1, 3):
             send(("gb", p, 0, by), spot(p), spot(p), neighbour(b, by))
+        for by in (1, 3):
+            send(("gc", p, 0, by), spot(p), spot(p), neighbour(c, by))
 
     def plane_group(p, m):
         a, b, c = axes[p]
@@ -431,8 +434,8 @@
             recv(("ga", p, 4 - k), block)
             for by in (1, 3):
                 send(("gb", p, k, by), block, block, neighbour(b, by))
-    for p in range(3):
-        plane_group(p, 0)
+            for by in (1, 3):
+                send(("gc", p, 0, by), block, block, neighbour(c, by))
     for k in (0, 1, 3, 2):
         for p in range(3):
             a, b, c = axes[p]
@@ -478,30 +481,36 @@
             return lax.rem(x_lo + by, 2)
         return shift(axes[p][2], by)
 
-    def multiply(p, by):
-        rows = users_of(p, by)
-        wide = rows.astype(F32)
-        totals["square"] = totals["square"] + jnp.sum(wide * wide, axis=0, keepdims=True)
-        weight = wts[p][plane_of(p, by)]
-        product = jnp.dot(weight.reshape(1024, weight.shape[-1]), rows, preferred_element_type=F32)
+    def multiply(*planes):
+        weights, rows = [], []
+        for p, by in planes:
+            block = users_of(p, by)
+            wide = block.astype(F32)
+            totals["square"] = totals["square"] + jnp.sum(wide * wide, axis=0, keepdims=True)
+            weight = wts[p][plane_of(p, by)]
+            weights.append(weight.reshape(1024, weight.shape[-1]))
+            rows.append(block)
+        if len(planes) > 1:
+            weights, rows = [jnp.concatenate(weights, axis=1)], [jnp.concatenate(rows, axis=0)]
+        product = jnp.dot(weights[0], rows[0], preferred_element_type=F32)
         if totals["first"]:
             gate_up[...] = product
         else:
             gate_up[...] += product
         totals["first"] = False
 
-    multiply(0, 0)
-    multiply(1, 0)
+    multiply((0, 0), (1, 0))
     for m in (1, 3, 2):
         pass_on(m)
-    for by in (1, 3):
-        multiply(0, by)
-        multiply(1, by)
-    multiply(2, 1)
-    for p in range(3):
-        a, b, c = axes[p]
+    multiply((0, 1), (0, 3))
+    multiply((1, 1), (1, 3))
+    multiply((2, 1),)
+    for p in range(2):
+        c = axes[p][2]
         recv(("gd", p), at(rts[p], **{c: shift(c, 2)}))
-        multiply(p, 2 if p < 2 else 0)
+    multiply((0, 2), (1, 2))
+    recv(("gd", 2), at(rts[2], x=shift("x", 2)))
+    multiply((2, 0),)
 
     scale = lax.rsqrt(totals["square"] * (1.0 / (32 * FEATS)) + norm_eps)
     for slot in range(2):
@@ -524,8 +533,8 @@
     def down(p, by):
         first, rows, _ = PARTS[p]
         j = plane_of(p, by)
-        product = jnp.dot(weight_plane(downt.at[0], p, j), act[0:256], preferred_element_type=F32)
-        product += jnp.dot(weight_plane(downt.at[1], p, j), act[256:512], preferred_element_type=F32)
+        weight = jnp.concatenate([weight_plane(downt.at[n], p, j) for n in range(2)], axis=1)
+        product = jnp.dot(weight, act[...], preferred_element_type=F32)
         product = (product * share).astype(BF16)
         for h in range(2):
             lanes = product[:, h * LANES : (h + 1) * LANES]
@@ -654,7 +663,7 @@
         pltpu.SemaphoreType.DMA((2, 2)),
         pltpu.SemaphoreType.DMA((9,)),
         pltpu.SemaphoreType.DMA((2, 6)),
-        pltpu.SemaphoreType.DMA((81,)),
+        pltpu.SemaphoreType.DMA((99,)),
         pltpu.SemaphoreType.DMA((134,)),
     ]
     gate_proj = gate_proj.reshape(2, 4, 4, FEATS, 256)

time: 104 us -> 101 us (0.971)
  Pallas kernels: 102 us -> 99 us
    pallas_call x1, Pallas kernels: 102 us -> 99 us  [body(): pl.pallas_call(layer_kernel, out_shape=(jax.ShapeDtypeStruct((FEATS, LANE...]
where the time goes in v4:
time: 101 us; the launch traced here: 100 us
  Pallas kernels  99 us (98%)
  local copies, waits for them, and re-layouts  1.45 us (1%)
    pallas_call x1, Pallas kernels, body(): pl.pallas_call(layer_kernel, out_shape=(jax.ShapeDtypeStruct((FEATS, LANE...  99 us

profile of v4, /device:TPU:0, one launch (start us, length us, event | category | flops | bytes accessed | tf_op | source)
XLA Modules:
  0.0 100.4 jit_solution(18176235919450373379)
XLA Ops:
  0.0 99.0 %shard_map.136 = (bf16[224,128]{1,0:T(8,128)(2,1)}, bf16[2,4,4,224,256]{4,3,2,1,0:T(8,128)(2,1)}, bf16[2,4,4,224,256]{4,3,2,1,0:T(8,128)(2,1)}, bf16[256,7168]{1,0:T(8,128)(2,1)}) custom-call(bf16[16,32,512]{2,1,0:T(8,128)(2,1)} %query_hbm.1, bf16[16,2048]{1,0:T(8,128)(2,1)} %rope_hbm.1, bf16[16,512,512]{2,1,0:T(8,128)(2,1)} %cache_hbm.1, ...), custom_call_target="tpu_custom_call" | custom-call | flops 8999999488 | bytes 28311552 | tf_op jit(solution)/shard_map/pallas_call | solution.py:672
  99.0 1.4 %copy.16 = bf16[128,224]{0,1:T(8,128)(2,1)} copy(bf16[128,224]{0,1:T(8,128)(2,1)} %bitcast.9) | data formatting | bytes 114688

commit v5 on v4

--- a/solution.py
+++ b/solution.py
@@ -47,7 +47,7 @@
     heads0, heads1, out_proj, attn, pair_in, far_in, far_out, hidden,
     weight_in, down_in, gain0, gain1, gain2, wt0, wt1, wt2, downt,
     rt0, rt1, rt2, gate_up, act, o0, o1, o2,
-    r1_0, r1_1, r1_2, r2_0, r2_1, r2_2, r3_0, r3_1, r3_2, r4_0, r4_1, r4_2, r5_0, r5_1, r5_2,
+    r1_0, r1_1, r1_2, r2_0, r2_1, r2_2, r5_0, r5_1, r5_2,
     kept, cache_sem, local_sem, stage_sem, send_sem, recv_sem,
 ):
     sec = lax.axis_index("sec")
@@ -60,16 +60,20 @@
         "z": lax.rem(dev, 4),
     }
 
-    def shift(axis, by):
-        return lax.rem(me[axis] + (by % 4), 4)
-
     def device(x, y, z, c):
         return ((x // 2) * 2 + c, lax.rem(x, 2) * 16 + y * 4 + z)
 
+    shifted = {(axis, by): lax.rem(me[axis] + by, 4) for axis in "xyz" for by in (1, 2, 3)}
+
+    def shift(axis, by):
+        return me[axis] if by % 4 == 0 else shifted[axis, by % 4]
+
+    def away(**by):
+        place = [shift(axis, by.get(axis, 0)) for axis in "xyz"]
+        return device(*place, core)
+
     def neighbour(axis, by):
-        place = dict(me)
-        place[axis] = shift(axis, by)
-        return device(place["x"], place["y"], place["z"], core)
+        return away(**{axis: by})
 
     partner = device(me["x"], me["y"], me["z"], 1 - core)
     x_lo_partner = (sec, (1 - x_lo) * 16 + me["y"] * 4 + me["z"])
@@ -101,7 +105,14 @@
         ).wait_recv()
 
 
-    around = [neighbour(axis, by) for axis in "xyz" for by in (1, 2, 3)] + [partner]
+    offsets = {}
+    for first, second in ("xy", "zx", "yz"):
+        for m in range(4):
+            for k in range(4):
+                offset = {"x": 0, "y": 0, "z": 0, first: k, second: m}
+                if k or m:
+                    offsets[tuple(offset.values())] = offset
+    around = [away(**offset) for offset in offsets.values()] + [partner]
     barrier = pltpu.get_barrier_semaphore()
     for other in around:
         pl.semaphore_signal(barrier, inc=1, device_id=other, device_id_type=MESH)
@@ -374,8 +385,8 @@
             for by in (1, 3):
                 region = head_slab(p, **{b: shift(b, m), c: shift(c, -by)})
                 recv(("hc", p, m, by), region)
-                if (m in (0, 1)) == (by == 1):
-                    send(("hd", p), region, region, neighbour(c, by))
+                passed = head_slab(p, **{"x": by // 2, b: shift(b, m), c: shift(c, -by)})
+                send(("hd", p), passed, passed, neighbour(c, by))
         work(2)
     work(len(tasks))
     project(0, 1)
@@ -414,18 +425,15 @@
     drain()
     for p in range(3):
         a, b, c = axes[p]
-        for by in (1, 3, 2):
-            send(("ga", p, by), spot(p), spot(p), neighbour(a, by))
-        for by in (1, 3):
-            send(("gb", p, 0, by), spot(p), spot(p), neighbour(b, by))
+        for k in (1, 3, 2):
+            send(("ga", p, k), spot(p), spot(p), away(**{a: k}))
         for by in (1, 3):
             send(("gc", p, 0, by), spot(p), spot(p), neighbour(c, by))
-
-    def plane_group(p, m):
-        a, b, c = axes[p]
-        slab = at(rts[p], **{b: shift(b, m), c: me[c]})
-        for by in (1, 3):
-            send(("gc", p, m, by), slab, slab, neighbour(c, by))
+    for m in (1, 3, 2):
+        for p in range(3):
+            a, b, c = axes[p]
+            for k in (0, 1, 3, 2):
+                send(("gb", p, m), spot(p), spot(p), away(**{a: k, b: m}))
 
     for k in (1, 3, 2):
         for p in range(3):
@@ -433,33 +441,25 @@
             block = spot(p, **{a: shift(a, k)})
             recv(("ga", p, 4 - k), block)
             for by in (1, 3):
-                send(("gb", p, k, by), block, block, neighbour(b, by))
-            for by in (1, 3):
                 send(("gc", p, 0, by), block, block, neighbour(c, by))
-    for k in (0, 1, 3, 2):
+    for m in (1, 3, 2):
         for p in range(3):
             a, b, c = axes[p]
+            slab = at(rts[p], **{b: shift(b, m), c: me[c]})
+            recv(("gb", p, 4 - m), slab)
             for by in (1, 3):
-                block = spot(p, **{a: shift(a, k), b: shift(b, -by)})
-                recv(("gb", p, k, by), block)
-                if (k in (0, 1)) == (by == 1):
-                    send(("gf", p), block, block, neighbour(b, by))
-    for p in range(3):
-        plane_group(p, 3)
-        plane_group(p, 1)
+                send(("gc", p, m, by), slab, slab, neighbour(c, by))
+
     def pass_on(m):
         for p in range(3):
             a, b, c = axes[p]
             for by in (1, 3):
                 region = at(rts[p], **{b: shift(b, m), c: shift(c, -by)})
                 recv(("gc", p, m, by), region)
-                if (m in (0, 1)) == (by == 1):
-                    send(("gd", p), region, region, neighbour(c, by))
-
-    for p in range(3):
-        a, b, c = axes[p]
-        recv(("gf", p), spot(p, **{a: slice(None), b: shift(b, 2)}))
-        plane_group(p, 2)
+                half_of = pl.ds(0, 2) if by == 1 else pl.ds(2, 2)
+                passed = at(rts[p], **{a: half_of, b: shift(b, m), c: shift(c, -by)})
+                send(("gd", p), passed, passed, neighbour(c, by))
+
     pass_on(0)
 
     totals = {"square": jnp.zeros((1, 256), F32), "first": True}
@@ -520,9 +520,7 @@
 
     drain()
     outs = (o0, o1, o2)
-    r1, r2, r3, r4, r5 = (
-        (r1_0, r1_1, r1_2), (r2_0, r2_1, r2_2), (r3_0, r3_1, r3_2), (r4_0, r4_1, r4_2), (r5_0, r5_1, r5_2)
-    )
+    r1, r2, r5 = (r1_0, r1_1, r1_2), (r2_0, r2_1, r2_2), (r5_0, r5_1, r5_2)
     share = jnp.sum(jnp.where(ids_ref[...] == dev, weights_ref[...], 0.0), axis=0, keepdims=True)
     share = jnp.where(
         core == 0,
@@ -590,38 +588,15 @@
             slab[...] = (
                 slab[...].astype(F32) + r2[p][m, 0].astype(F32) + r2[p][m, 1].astype(F32)
             ).astype(BF16)
-            if m == 2:
-                send(("s3", p, 0), slab.at[0:2], r3[p].at[0:2], neighbour(b, 1))
-                send(("s3", p, 1), slab.at[2:4], r3[p].at[2:4], neighbour(b, 3))
-            elif m == 1:
-                send(("s4", p), slab.at[2:4], r4[p].at[0, 2:4], neighbour(b, 1))
-            elif m == 3:
-                send(("s4", p), slab.at[0:2], r4[p].at[1, 0:2], neighbour(b, 3))
-    for p in range(3):
-        a, b, c = axes[p]
-        recv(("s3", p, 0), r3[p].at[0:2])
-        slab = o_slab(p, 0, 1).at[0:2]
-        add_to(slab, r3[p].at[0:2])
-        send(("s4", p), slab, r4[p].at[0, 0:2], neighbour(b, 1))
-        recv(("s3", p, 1), r3[p].at[2:4])
-        slab = o_slab(p, 0, 3).at[2:4]
-        add_to(slab, r3[p].at[2:4])
-        send(("s4", p), slab, r4[p].at[1, 2:4], neighbour(b, 3))
-    for p in range(3):
-        a, b, c = axes[p]
-        recv(("s4", p), r4[p])
-        slab = o_slab(p, 0, 0)
-        slab[...] = (
-            slab[...].astype(F32) + r4[p][0].astype(F32) + r4[p][1].astype(F32)
-        ).astype(BF16)
-        for k in (2, 1, 3):
-            send(("s5", p), slab.at[shift(a, k)], r5[p].at[k - 1], neighbour(a, k))
+            for k in (2, 1, 3, 0):
+                if k or m:
+                    send(("s5", p), slab.at[shift(a, k)], r5[p].at[4 * m + k - 1], away(**{a: k, b: m}))
     for p, (first, rows, _) in enumerate(PARTS):
         a = axes[p][0]
         total = kept[first : first + rows, :] + outs[p][me["x"], me["y"], me["z"]].astype(F32)
         recv(("s5", p), r5[p])
-        for k in (1, 3, 2):
-            total = total + r5[p][k - 1].astype(F32)
+        for n in range(15):
+            total = total + r5[p][n].astype(F32)
         out_ref[first : first + rows, :] = total.astype(BF16)
     drain()
 
@@ -656,15 +631,13 @@
         *[bf(4, 4, 4, r, LANES) for r in rows],
         *[bf(4, 4, r, LANES) for r in rows],
         *[bf(4, 2, 4, r, LANES) for r in rows],
-        *[bf(4, r, LANES) for r in rows],
-        *[bf(2, 4, r, LANES) for r in rows],
-        *[bf(3, r, LANES) for r in rows],
+        *[bf(15, r, LANES) for r in rows],
         f32(FEATS, LANES),
         pltpu.SemaphoreType.DMA((2, 2)),
         pltpu.SemaphoreType.DMA((9,)),
         pltpu.SemaphoreType.DMA((2, 6)),
-        pltpu.SemaphoreType.DMA((99,)),
-        pltpu.SemaphoreType.DMA((134,)),
+        pltpu.SemaphoreType.DMA((111,)),
+        pltpu.SemaphoreType.DMA((107,)),
     ]
     gate_proj = gate_proj.reshape(2, 4, 4, FEATS, 256)
     up_proj = up_proj.reshape(2, 4, 4, FEATS, 256)

time: 101 us -> 99.4 us (0.984)
  Pallas kernels: 99 us -> 97.7 us
    pallas_call x1, Pallas kernels: 99 us -> 97.7 us  [body(): pl.pallas_call(layer_kernel, out_shape=(jax.ShapeDtypeStruct((FEATS, LANE...]
where the time goes in v5:
time: 99.4 us; the launch traced here: 99.1 us
  Pallas kernels  97.7 us (98%)
  local copies, waits for them, and re-layouts  1.45 us (1%)
    pallas_call x1, Pallas kernels, body(): pl.pallas_call(layer_kernel, out_shape=(jax.ShapeDtypeStruct((FEATS, LANE...  97.7 us

profile of v5, /device:TPU:0, one launch (start us, length us, event | category | flops | bytes accessed | tf_op | source)
XLA Modules:
  0.0 99.1 jit_solution(7814016783774650035)
XLA Ops:
  0.0 97.7 %shard_map.136 = (bf16[224,128]{1,0:T(8,128)(2,1)}, bf16[2,4,4,224,256]{4,3,2,1,0:T(8,128)(2,1)}, bf16[2,4,4,224,256]{4,3,2,1,0:T(8,128)(2,1)}, bf16[256,7168]{1,0:T(8,128)(2,1)}) custom-call(bf16[16,32,512]{2,1,0:T(8,128)(2,1)} %query_hbm.1, bf16[16,2048]{1,0:T(8,128)(2,1)} %rope_hbm.1, bf16[16,512,512]{2,1,0:T(8,128)(2,1)} %cache_hbm.1, ...), custom_call_target="tpu_custom_call" | custom-call | flops 8999999488 | bytes 28311552 | tf_op jit(solution)/shard_map/pallas_call | solution.py:645
  97.7 1.4 %copy.16 = bf16[128,224]{0,1:T(8,128)(2,1)} copy(bf16[128,224]{0,1:T(8,128)(2,1)} %bitcast.9) | data formatting | bytes 114688

commit v6 on v5

--- a/solution.py
+++ b/solution.py
@@ -52,25 +52,29 @@
 ):
     sec = lax.axis_index("sec")
     dev = lax.axis_index("dev")
-    x_hi, core = sec // 2, lax.rem(sec, 2)
-    x_lo = dev // 16
+    x_hi, core = lax.div(sec, 2), lax.rem(sec, 2)
+    x_lo = lax.div(dev, 16)
     me = {
         "x": x_hi * 2 + x_lo,
-        "y": lax.rem(dev // 4, 4),
+        "y": lax.rem(lax.div(dev, 4), 4),
         "z": lax.rem(dev, 4),
     }
 
     def device(x, y, z, c):
-        return ((x // 2) * 2 + c, lax.rem(x, 2) * 16 + y * 4 + z)
+        return (lax.div(x, 2) * 2 + c, lax.rem(x, 2) * 16 + y * 4 + z)
 
     shifted = {(axis, by): lax.rem(me[axis] + by, 4) for axis in "xyz" for by in (1, 2, 3)}
 
     def shift(axis, by):
         return me[axis] if by % 4 == 0 else shifted[axis, by % 4]
 
+    ids = {}
+
     def away(**by):
-        place = [shift(axis, by.get(axis, 0)) for axis in "xyz"]
-        return device(*place, core)
+        offset = tuple(by.get(axis, 0) for axis in "xyz")
+        if offset not in ids:
+            ids[offset] = device(*[shift(axis, n) for axis, n in zip("xyz", offset)], core)
+        return ids[offset]
 
     def neighbour(axis, by):
         return away(**{axis: by})
@@ -79,6 +83,7 @@
     x_lo_partner = (sec, (1 - x_lo) * 16 + me["y"] * 4 + me["z"])
 
     tags = {}
+    kinds = {}
     sent = []
 
     def number(tag):
@@ -86,16 +91,33 @@
 
     def send(tag, src, dst, to):
         i = number(tag)
+        kind = tag[:2]
         copy = pltpu.make_async_remote_copy(
-            src_ref=src, dst_ref=dst, send_sem=send_sem.at[len(sent)], recv_sem=recv_sem.at[i],
-            device_id=to, device_id_type=MESH,
+            src_ref=src, dst_ref=dst, send_sem=send_sem.at[kinds.setdefault(kind, len(kinds))],
+            recv_sem=recv_sem.at[i], device_id=to, device_id_type=MESH,
         )
         copy.start()
-        sent.append(copy)
+        sent.append((kind, copy))
 
     def drain():
-        while sent:
-            sent.pop().wait_send()
+        blocks = dict(hb=4, hf=2, hc=16, hd=8, ga=3, gb=12, gc=32, gd=16, s1=16, s2=32, s5=15)
+        alone = {kind: copy for kind, copy in sent}
+        for kind, i in kinds.items():
+            if kind[0] not in blocks:
+                alone[kind].wait_send()
+                continue
+            p = kind[1]
+            held = heads[p] if kind[0][0] == "h" else rts[p]
+            views = {
+                2: lambda: held.at[:, 0, 0], 3: lambda: held.at[0, 0, 0:3], 4: lambda: held.at[0, 0],
+                8: lambda: held.at[0, 0:2], 12: lambda: held.at[0, 0:3], 15: lambda: r5[p],
+                16: lambda: held.at[0], 32: lambda: held.at[0:2],
+            }
+            view = views[blocks[kind[0]]]()
+            pltpu.make_async_remote_copy(
+                src_ref=view, dst_ref=view, send_sem=send_sem.at[i], recv_sem=recv_sem.at[0],
+                device_id=partner, device_id_type=MESH,
+            ).wait_send()
 
     def recv(tag, region):
         i = number(tag)
@@ -118,6 +140,8 @@
         pl.semaphore_signal(barrier, inc=1, device_id=other, device_id_type=MESH)
 
     heads = (heads0, heads1)
+    rts = (rt0, rt1, rt2)
+    r1, r2, r5 = (r1_0, r1_1, r1_2), (r2_0, r2_1, r2_2), (r5_0, r5_1, r5_2)
     half = heads0.shape[-1]
     own_heads = [at(h, x=x_lo, y=me["y"], z=me["z"]) for h in heads]
     my_hidden = hidden_hbm.at[:, pl.ds(pl.multiple_of(sec * LANES, LANES), LANES)]
@@ -412,7 +436,6 @@
     kept[...] = residual
     routed = residual.astype(BF16)
 
-    rts = (rt0, rt1, rt2)
     for p, (first, rows, _) in enumerate(PARTS):
         rts[p][me["x"], me["y"], me["z"]] = routed[first : first + rows]
 
@@ -422,24 +445,23 @@
         return at(rts[p], **place)
 
     axes = [tuple(o) for _, _, o in PARTS]
-    drain()
     for p in range(3):
         a, b, c = axes[p]
         for k in (1, 3, 2):
             send(("ga", p, k), spot(p), spot(p), away(**{a: k}))
         for by in (1, 3):
             send(("gc", p, 0, by), spot(p), spot(p), neighbour(c, by))
-    for m in (1, 3, 2):
-        for p in range(3):
-            a, b, c = axes[p]
-            for k in (0, 1, 3, 2):
-                send(("gb", p, m), spot(p), spot(p), away(**{a: k, b: m}))
-
+    for p in range(3):
+        a, b, c = axes[p]
+        for m in (2, 1, 3):
+            send(("gb", p, m), spot(p), spot(p), away(**{b: m}))
     for k in (1, 3, 2):
         for p in range(3):
             a, b, c = axes[p]
             block = spot(p, **{a: shift(a, k)})
             recv(("ga", p, 4 - k), block)
+            for m in (2, 1, 3):
+                send(("gb", p, m), block, block, away(**{b: m}))
             for by in (1, 3):
                 send(("gc", p, 0, by), block, block, neighbour(c, by))
     for m in (1, 3, 2):
@@ -518,9 +540,7 @@
         upward = gate_up[slot * 512 + 256 : slot * 512 + 512] * scale
         act[slot * 256 : slot * 256 + 256] = (gate / (1.0 + jnp.exp(-gate)) * upward).astype(BF16)
 
-    drain()
     outs = (o0, o1, o2)
-    r1, r2, r5 = (r1_0, r1_1, r1_2), (r2_0, r2_1, r2_2), (r5_0, r5_1, r5_2)
     share = jnp.sum(jnp.where(ids_ref[...] == dev, weights_ref[...], 0.0), axis=0, keepdims=True)
     share = jnp.where(
         core == 0,
@@ -636,7 +656,7 @@
         pltpu.SemaphoreType.DMA((2, 2)),
         pltpu.SemaphoreType.DMA((9,)),
         pltpu.SemaphoreType.DMA((2, 6)),
-        pltpu.SemaphoreType.DMA((111,)),
+        pltpu.SemaphoreType.DMA((36,)),
         pltpu.SemaphoreType.DMA((107,)),
     ]
     gate_proj = gate_proj.reshape(2, 4, 4, FEATS, 256)

time: 99.4 us -> 97.1 us (0.977)
  Pallas kernels: 97.7 us -> 95.4 us
    pallas_call x1, Pallas kernels: 97.7 us -> 95.4 us  [body(): pl.pallas_call(layer_kernel, out_shape=(jax.ShapeDtypeStruct((FEATS, LANE...]
where the time goes in v6:
time: 97.1 us; the launch traced here: 96.9 us
  Pallas kernels  95.4 us (98%)
  local copies, waits for them, and re-layouts  1.45 us (1%)
    pallas_call x1, Pallas kernels, body(): pl.pallas_call(layer_kernel, out_shape=(jax.ShapeDtypeStruct((FEATS, LANE...  95.4 us

profile of v6, /device:TPU:0, one launch (start us, length us, event | category | flops | bytes accessed | tf_op | source)
XLA Modules:
  0.0 96.9 jit_solution(7766652974797520011)
XLA Ops:
  0.0 95.4 %shard_map.136 = (bf16[224,128]{1,0:T(8,128)(2,1)}, bf16[2,4,4,224,256]{4,3,2,1,0:T(8,128)(2,1)}, bf16[2,4,4,224,256]{4,3,2,1,0:T(8,128)(2,1)}, bf16[256,7168]{1,0:T(8,128)(2,1)}) custom-call(bf16[16,32,512]{2,1,0:T(8,128)(2,1)} %query_hbm.1, bf16[16,2048]{1,0:T(8,128)(2,1)} %rope_hbm.1, bf16[16,512,512]{2,1,0:T(8,128)(2,1)} %cache_hbm.1, ...), custom_call_target="tpu_custom_call" | custom-call | flops 8999999488 | bytes 28311552 | tf_op jit(solution)/shard_map/pallas_call | solution.py:665
  95.5 1.4 %copy.16 = bf16[128,224]{0,1:T(8,128)(2,1)} copy(bf16[128,224]{0,1:T(8,128)(2,1)} %bitcast.9) | data formatting | bytes 114688

commit v7 on v6

--- a/solution.py
+++ b/solution.py
@@ -350,14 +350,34 @@
             task()
         del tasks[:count]
 
-    work(8)
-
-    def slab_sends(p, m):
+    work(4)
+
+    def onward(p, m, k):
         b, c = order[p]
-        slab = head_slab(p, **{b: shift(b, m), c: me[c]})
+        block = head_block(p, k, **{b: shift(b, m)})
         for by in (1, 3):
-            send(("hc", p, m, by), slab, slab, neighbour(c, by))
-
+            send(("hc", p, m, by), block, block, neighbour(c, by))
+
+    def from_sides(k):
+        for p in range(2):
+            b, c = order[p]
+            for m, by in ((3, 1), (1, 3)) if k == 0 else ((1, 3), (3, 1)):
+                block = head_block(p, k, **{b: shift(b, m)})
+                recv(("hb", p, k, by), block)
+                if (by == 1) == (k == 0):
+                    send(("hf", p, k), block, block, neighbour(b, by))
+        for p in range(2):
+            for m in (3, 1):
+                onward(p, m, k)
+
+    def from_opposite(k):
+        for p in range(2):
+            b, c = order[p]
+            recv(("hf", p, k), head_block(p, k, **{b: shift(b, 2)}))
+            onward(p, 2, k)
+
+    from_sides(0)
+    work(2)
     for p in range(2):
         b, c = order[p]
         other = head_block(p, 1)
@@ -365,27 +385,11 @@
         for by in (1, 3):
             send(("hb", p, 1, by), other, other, neighbour(b, by))
     for p in range(2):
-        other = head_block(p, 1)
-        for by in (1, 3):
-            send(("hc", p, 0, by), other, other, neighbour(order[p][1], by))
-    for p in range(2):
-        b, c = order[p]
-        block = head_block(p, 0, **{b: shift(b, 3)})
-        recv(("hb", p, 0, 1), block)
-        send(("hf", p), block, block, neighbour(b, 1))
-        recv(("hb", p, 0, 3), head_block(p, 0, **{b: shift(b, 1)}))
-    for p in range(2):
-        b, c = order[p]
-        block = head_block(p, 1, **{b: shift(b, 1)})
-        recv(("hb", p, 1, 3), block)
-        send(("hf", p), block, block, neighbour(b, 3))
-        slab_sends(p, 1)
-        recv(("hb", p, 1, 1), head_block(p, 1, **{b: shift(b, 3)}))
-        slab_sends(p, 3)
-    for p in range(2):
-        b, c = order[p]
-        recv(("hf", p), head_slab(p, **{b: shift(b, 2), c: me[c]}))
-        slab_sends(p, 2)
+        onward(p, 0, 1)
+    from_opposite(0)
+    work(2)
+    from_sides(1)
+    from_opposite(1)
     fetch_partner()
 
     def project(p, by, first=False):
@@ -657,7 +661,7 @@
         pltpu.SemaphoreType.DMA((9,)),
         pltpu.SemaphoreType.DMA((2, 6)),
         pltpu.SemaphoreType.DMA((36,)),
-        pltpu.SemaphoreType.DMA((107,)),
+        pltpu.SemaphoreType.DMA((109,)),
     ]
     gate_proj = gate_proj.reshape(2, 4, 4, FEATS, 256)
     up_proj = up_proj.reshape(2, 4, 4, FEATS, 256)

time: 97.1 us -> 97.3 us (level)
  no operation moved by 1% of the time
where the time goes in v7:
time: 97.3 us; the launch traced here: 97 us
  Pallas kernels  95.5 us (98%)
  local copies, waits for them, and re-layouts  1.45 us (1%)
    pallas_call x1, Pallas kernels, body(): pl.pallas_call(layer_kernel, out_shape=(jax.ShapeDtypeStruct((FEATS, LANE...  95.5 us

profile of v7, /device:TPU:0, one launch (start us, length us, event | category | flops | bytes accessed | tf_op | source)
XLA Modules:
  0.0 97.0 jit_solution(1459347314348933821)
XLA Ops:
  0.0 95.5 %shard_map.136 = (bf16[224,128]{1,0:T(8,128)(2,1)}, bf16[2,4,4,224,256]{4,3,2,1,0:T(8,128)(2,1)}, bf16[2,4,4,224,256]{4,3,2,1,0:T(8,128)(2,1)}, bf16[256,7168]{1,0:T(8,128)(2,1)}) custom-call(bf16[16,32,512]{2,1,0:T(8,128)(2,1)} %query_hbm.1, bf16[16,2048]{1,0:T(8,128)(2,1)} %rope_hbm.1, bf16[16,512,512]{2,1,0:T(8,128)(2,1)} %cache_hbm.1, ...), custom_call_target="tpu_custom_call" | custom-call | flops 8999999488 | bytes 28311552 | tf_op jit(solution)/shard_map/pallas_call | solution.py:669
  95.6 1.4 %copy.16 = bf16[128,224]{0,1:T(8,128)(2,1)} copy(bf16[128,224]{0,1:T(8,128)(2,1)} %bitcast.9) | data formatting | bytes 114688

commit v8 on v7

--- a/solution.py
+++ b/solution.py
@@ -17,6 +17,7 @@
 PARTS = ((0, 80, "xyz"), (80, 80, "zxy"), (160, 64, "yzx"))
 FEATS = 224
 LANES = 128
+LATE = 640
 GROUP = 4
 
 
@@ -91,7 +92,7 @@
 
     def send(tag, src, dst, to):
         i = number(tag)
-        kind = tag[:2]
+        kind = tag[: 3 if tag[0] in ("hb", "hf", "hc", "hd") else 2]
         copy = pltpu.make_async_remote_copy(
             src_ref=src, dst_ref=dst, send_sem=send_sem.at[kinds.setdefault(kind, len(kinds))],
             recv_sem=recv_sem.at[i], device_id=to, device_id_type=MESH,
@@ -100,7 +101,7 @@
         sent.append((kind, copy))
 
     def drain():
-        blocks = dict(hb=4, hf=2, hc=16, hd=8, ga=3, gb=12, gc=32, gd=16, s1=16, s2=32, s5=15)
+        blocks = dict(hb=2, hc=8, hd=4, hl=16, ga=3, gb=12, gc=32, gd=16, s1=16, s2=32, s5=15)
         alone = {kind: copy for kind, copy in sent}
         for kind, i in kinds.items():
             if kind[0] not in blocks:
@@ -114,6 +115,10 @@
                 16: lambda: held.at[0], 32: lambda: held.at[0:2],
             }
             view = views[blocks[kind[0]]]()
+            if kind[0] == "hl":
+                view = late(view)
+            elif kind[0][0] == "h" and kind[2] == 1:
+                view = early(view)
             pltpu.make_async_remote_copy(
                 src_ref=view, dst_ref=view, send_sem=send_sem.at[i], recv_sem=recv_sem.at[0],
                 device_id=partner, device_id_type=MESH,
@@ -268,10 +273,16 @@
 
     order = (("y", "z"), ("z", "y"))
 
+    def early(ref):
+        return ref.at[(slice(None),) * (len(ref.shape) - 1) + (pl.ds(0, half - LATE),)]
+
+    def late(ref):
+        return ref.at[(slice(None),) * (len(ref.shape) - 1) + (pl.ds(half - LATE, LATE),)]
+
     def head_block(p, k, **index):
         place = {"x": lax.rem(x_lo + k, 2), "y": me["y"], "z": me["z"]}
         place.update(index)
-        return at(heads[p], **place)
+        return early(at(heads[p], **place)) if k else at(heads[p], **place)
 
     def head_slab(p, **index):
         return at(heads[p], **index)
@@ -279,12 +290,12 @@
     for p in range(2):
         for h in range(heads_here // 2):
             heads[p][x_lo, me["y"], me["z"], :, h * 128 : h * 128 + 128] = head_value(p * (heads_here // 2) + h)
-        send(("hx", p), own_heads[p], own_heads[p], x_lo_partner)
+        send(("hx", p), early(own_heads[p]), early(own_heads[p]), x_lo_partner)
         b, c = order[p]
         for by in (1, 3):
             send(("hb", p, 0, by), own_heads[p], own_heads[p], neighbour(b, by))
         for by in (1, 3):
-            send(("hc", p, 0, by), own_heads[p], own_heads[p], neighbour(c, by))
+            send(("hc", p, 0, 0, by), own_heads[p], own_heads[p], neighbour(c, by))
 
     wts = (wt0, wt1, wt2)
     gains = (gain0, gain1, gain2)
@@ -356,7 +367,7 @@
         b, c = order[p]
         block = head_block(p, k, **{b: shift(b, m)})
         for by in (1, 3):
-            send(("hc", p, m, by), block, block, neighbour(c, by))
+            send(("hc", p, k, m, by), block, block, neighbour(c, by))
 
     def from_sides(k):
         for p in range(2):
@@ -405,26 +416,57 @@
         else:
             attn[:, j] += product
 
-    loads[4].wait()
-    project(0, 0)
-    for m in (0, 1, 3, 2):
+    def plane_late(p, by, k):
+        c = order[p][1]
+        return late(at(heads[p], **{"x": lax.rem(x_lo + k, 2), c: shift(c, by)}))
+
+    def cross(*planes):
+        for by in planes:
+            for p in range(2):
+                mine = plane_late(p, by, 0)
+                send(("hl", p, by), mine, mine, x_lo_partner)
+
+    def take(m, k):
         for p in range(2):
             b, c = order[p]
             for by in (1, 3):
-                region = head_slab(p, **{b: shift(b, m), c: shift(c, -by)})
-                recv(("hc", p, m, by), region)
-                passed = head_slab(p, **{"x": by // 2, b: shift(b, m), c: shift(c, -by)})
-                send(("hd", p), passed, passed, neighbour(c, by))
-        work(2)
+                block = head_block(p, k, **{b: shift(b, m), c: shift(c, -by)})
+                recv(("hc", p, k, m, by), block)
+                if (by == 1) == (p == k):
+                    send(("hd", p, k), block, block, neighbour(c, by))
+
+    def opposite(p, k):
+        c = order[p][1]
+        block = at(heads[p], **{"x": lax.rem(x_lo + k, 2), c: shift(c, 2)})
+        recv(("hd", p, k), early(block) if k else block)
+
+    def finished(p, by):
+        recv(("hl", p, by), plane_late(p, by, 1))
+        project(p, by)
+
+    cross(0)
+    loads[4].wait()
+    for m, k in ((0, 0), (3, 0), (1, 0), (0, 1)):
+        take(m, k)
+        work(1)
+    take(2, 0)
+    cross(1, 3)
+    work(2)
+    take(1, 1)
+    take(3, 1)
+    for p in range(2):
+        opposite(p, 0)
+    cross(2)
+    take(2, 1)
     work(len(tasks))
-    project(0, 1)
-    project(0, 3)
-    recv(("hd", 0), head_slab(0, **{order[0][1]: shift(order[0][1], 2)}))
-    project(0, 2)
     for by in (0, 1, 3):
-        project(1, by)
-    recv(("hd", 1), head_slab(1, **{order[1][1]: shift(order[1][1], 2)}))
-    project(1, 2)
+        finished(0, by)
+    opposite(0, 1)
+    finished(0, 2)
+    for by in (0, 1, 3):
+        finished(1, by)
+    opposite(1, 1)
+    finished(1, 2)
 
     attn_mine = attn.at[:, pl.ds(core * 2, 2)]
     send(("pair",), attn.at[:, pl.ds((1 - core) * 2, 2)], pair_in, partner)
@@ -660,8 +702,8 @@
         pltpu.SemaphoreType.DMA((2, 2)),
         pltpu.SemaphoreType.DMA((9,)),
         pltpu.SemaphoreType.DMA((2, 6)),
-        pltpu.SemaphoreType.DMA((36,)),
-        pltpu.SemaphoreType.DMA((109,)),
+        pltpu.SemaphoreType.DMA((46,)),
+        pltpu.SemaphoreType.DMA((135,)),
     ]
     gate_proj = gate_proj.reshape(2, 4, 4, FEATS, 256)
     up_proj = up_proj.reshape(2, 4, 4, FEATS, 256)

time: 97.3 us -> 101 us (1.038)
  Pallas kernels: 95.5 us -> 99.7 us
    pallas_call x1, Pallas kernels: 95.5 us -> 99.7 us  [body(): pl.pallas_call(layer_kernel, out_shape=(jax.ShapeDtypeStruct((FEATS, LANE...]
where the time goes in v8:
time: 101 us
  Pallas kernels  99.7 us (99%)
  local copies, waits for them, and re-layouts  1.45 us (1%)
    pallas_call x1, Pallas kernels, body(): pl.pallas_call(layer_kernel, out_shape=(jax.ShapeDtypeStruct((FEATS, LANE...  99.7 us

profile of v8, /device:TPU:0, one launch (start us, length us, event | category | flops | bytes accessed | tf_op | source)
XLA Modules:
  0.0 101.1 jit_solution(12329222818494566579)
XLA Ops:
  0.0 99.7 %shard_map.136 = (bf16[224,128]{1,0:T(8,128)(2,1)}, bf16[2,4,4,224,256]{4,3,2,1,0:T(8,128)(2,1)}, bf16[2,4,4,224,256]{4,3,2,1,0:T(8,128)(2,1)}, bf16[256,7168]{1,0:T(8,128)(2,1)}) custom-call(bf16[16,32,512]{2,1,0:T(8,128)(2,1)} %query_hbm.1, bf16[16,2048]{1,0:T(8,128)(2,1)} %rope_hbm.1, bf16[16,512,512]{2,1,0:T(8,128)(2,1)} %cache_hbm.1, ...), custom_call_target="tpu_custom_call" | custom-call | flops 8999999488 | bytes 28311552 | tf_op jit(solution)/shard_map/pallas_call | solution.py:711
  99.7 1.4 %copy.16 = bf16[128,224]{0,1:T(8,128)(2,1)} copy(bf16[128,224]{0,1:T(8,128)(2,1)} %bitcast.9) | data formatting | bytes 114688

commit v9 on v6

--- a/solution.py
+++ b/solution.py
@@ -570,7 +570,7 @@
     for p in range(3):
         c = axes[p][2]
         down(p, 2 if p < 2 else 0)
-        for m in (2, 0, 3, 1):
+        for m in (2, 1, 3, 0):
             by = 1 if m in (0, 1) else 3
             send(("s1", p, m), o_slab(p, 2, m), r1[p].at[m], neighbour(c, by))
     for p in range(3):

time: 97.1 us -> 97.2 us (level)
  no operation moved by 1% of the time
where the time goes in v9:
time: 97.2 us; the launch traced here: 96.9 us
  Pallas kernels  95.5 us (98%)
  local copies, waits for them, and re-layouts  1.45 us (1%)
    pallas_call x1, Pallas kernels, body(): pl.pallas_call(layer_kernel, out_shape=(jax.ShapeDtypeStruct((FEATS, LANE...  95.5 us

profile of v9, /device:TPU:0, one launch (start us, length us, event | category | flops | bytes accessed | tf_op | source)
XLA Modules:
  0.0 96.9 jit_solution(14680000559961882280)
XLA Ops:
  0.0 95.5 %shard_map.136 = (bf16[224,128]{1,0:T(8,128)(2,1)}, bf16[2,4,4,224,256]{4,3,2,1,0:T(8,128)(2,1)}, bf16[2,4,4,224,256]{4,3,2,1,0:T(8,128)(2,1)}, bf16[256,7168]{1,0:T(8,128)(2,1)}) custom-call(bf16[16,32,512]{2,1,0:T(8,128)(2,1)} %query_hbm.1, bf16[16,2048]{1,0:T(8,128)(2,1)} %rope_hbm.1, bf16[16,512,512]{2,1,0:T(8,128)(2,1)} %cache_hbm.1, ...), custom_call_target="tpu_custom_call" | custom-call | flops 8999999488 | bytes 28311552 | tf_op jit(solution)/shard_map/pallas_call | solution.py:665
  95.5 1.4 %copy.16 = bf16[128,224]{0,1:T(8,128)(2,1)} copy(bf16[128,224]{0,1:T(8,128)(2,1)} %bitcast.9) | data formatting | bytes 114688
